TPU v7x, 32 devices: a whole 2x2x4 slice. The times are simulated.
32 devices in a mesh: section: 4 (over z), ep: 8 (over y, x, core).
Axes of the slice: x: 2, y: 2, z: 4, core: 2. Of those that a mesh axis runs over, the one named last changes fastest.
Arguments:
- fresh_tokens: bfloat16 [128, 3584], P('ep'), may hold values from -6 to 6
- sent_forward: bfloat16 [4, 128, 3584], P('section', 'ep'), may hold values from -6 to 6
- sent_backward: bfloat16 [4, 128, 3584], P('section', 'ep'), may hold values from -1.1953125 to 1.1953125
- turn_gradient: bfloat16 [128, 3584], P('ep'), may hold values from -1.1953125 to 1.1953125
- saved_input: bfloat16 [4, 128, 3584], P('section', 'ep'), may hold values from -6 to 6
- gain: bfloat16 [4, 3584], P('section'), may hold values from 0.5 to 1.5
- ids_front: int32 [4, 128, 2], P('section', 'ep'), may hold values from 0 to 7, all different within a row; in each aligned block of 16 rows (0 to 15, 16 to 31, ..., all dimensions but the last counted through in order) at most 8 rows name the same one
- affinity_front: float32 [4, 128, 2], P('section', 'ep'), may hold values from 0.1 to 1
- ids_back: int32 [4, 128, 2], P('section', 'ep'), may hold values from 0 to 7, all different within a row; in each aligned block of 16 rows (0 to 15, 16 to 31, ..., all dimensions but the last counted through in order) at most 8 rows name the same one
- affinity_back: float32 [4, 128, 2], P('section', 'ep'), may hold values from 0.1 to 1
- w_gate: bfloat16 [4, 3584, 8192], P('section', None, 'ep'), may hold values from -0.09375 to 0.09375
- w_up: bfloat16 [4, 3584, 8192], P('section', None, 'ep'), may hold values from -0.09375 to 0.09375
- w_down: bfloat16 [4, 8192, 3584], P('section', 'ep'), may hold values from -0.1875 to 0.1875
- mirror_gate: bfloat16 [4, 3584, 8192], P('section', None, 'ep'), may hold values from -6 to 6
- mirror_up: bfloat16 [4, 3584, 8192], P('section', None, 'ep'), may hold values from -6 to 6
- mirror_down: bfloat16 [4, 8192, 3584], P('section', 'ep'), may hold values from -6 to 6
Outputs:
- forward_out: bfloat16 [4, 128, 3584], P('section', 'ep')
- grad_input: bfloat16 [4, 128, 3584], P('section', 'ep')
- grad_gate: bfloat16 [4, 3584, 8192], P('section', None, 'ep')
- grad_up: bfloat16 [4, 3584, 8192], P('section', None, 'ep')
- grad_down: bfloat16 [4, 8192, 3584], P('section', 'ep')
Inputs may be any that keep to these rules, and one draw needn't show every extreme that they name: `ids_front`: each row names 2 different experts. In each aligned block of 16 rows (the rows of one device) no expert is named by more than 8 rows, a bound that some block reaches. `ids_back`: each row names 2 different experts. In each aligned block of 16 rows (the rows of one device) no expert is named by more than 8 rows, a bound that some block reaches.
All inputs are finite; a program needn't handle non-finite values.
Results may differ from a plain program's by a relative error of at most 0.0068.
Values may be sent and summed in bfloat16 or wider, within the bound.
No kernel may reach another device: no remote copies, remote signals or barrier semaphores. Data moves between devices by JAX's collectives and lax.ppermute only.
A program may use at most 128 MiB of HBM per device.

v0:
```python
import jax
import jax.numpy as jnp
from jax import lax
from jax.sharding import PartitionSpec as P

EXPERTS = 8


highest = lax.Precision.HIGHEST


def passed_along(value, axis, by):
    peers = lax.axis_size(axis)
    pairs = [(i, i + by) for i in range(peers) if 0 <= i + by < peers]
    return lax.ppermute(value, axis, pairs)


def silu_of(pre_act):
    return pre_act * jax.nn.sigmoid(pre_act)


def norm_rows(inputs, gain):
    values = inputs.astype(jnp.float32)
    inverse = lax.rsqrt(jnp.mean(values * values, axis=-1, keepdims=True) + 1e-06)
    normed = (values * inverse * gain.astype(jnp.float32)).astype(jnp.bfloat16)
    return (values, inverse, normed)


def slot_tables(route_ids, affinity, capacity):
    flat_ids = route_ids.reshape(-1)
    onehot = (flat_ids[:, None] == jnp.arange(EXPERTS, dtype=jnp.int32)[None, :]).astype(jnp.int32)
    earlier = jnp.cumsum(onehot, axis=0) - onehot
    position = jnp.sum(earlier * onehot, axis=1)
    target = (flat_ids * capacity + position).reshape(route_ids.shape)
    columns = jnp.arange(EXPERTS * capacity, dtype=jnp.int32)
    matches = (target[:, :, None] == columns[None, None, :]).astype(jnp.float32)
    shares = affinity / jnp.sum(affinity, axis=1, keepdims=True)
    return (jnp.sum(matches, axis=1), jnp.sum(matches * shares[:, :, None], axis=1))


def to_experts(packed, groups):
    row_width = packed.shape[-1]
    capacity = packed.shape[0] // EXPERTS
    sending = jnp.broadcast_to(
        packed.reshape(EXPERTS, 1, capacity, row_width), (EXPERTS, groups, capacity, row_width)
    )
    gathered = lax.all_to_all(
        sending.reshape(EXPERTS * groups, capacity, row_width),
        "ep",
        split_axis=0,
        concat_axis=0,
        tiled=True,
    )
    return gathered


def from_experts(partial_value, groups):
    sources, capacity, row_width = partial_value.shape
    returned_rows = lax.all_to_all(partial_value, "ep", split_axis=0, concat_axis=0, tiled=True)
    summed = jnp.sum(
        returned_rows.astype(jnp.float32).reshape(EXPERTS, groups, capacity, row_width), axis=1
    )
    return summed.reshape(EXPERTS * capacity, row_width)


def expert_partial(token_rows, gate_cols, up_cols, down_rows):
    gate_pre = jnp.dot(token_rows, gate_cols, preferred_element_type=jnp.float32)
    up_pre = jnp.dot(token_rows, up_cols, preferred_element_type=jnp.float32)
    hidden = (silu_of(gate_pre) * up_pre).astype(jnp.bfloat16)
    return jnp.dot(hidden, down_rows, preferred_element_type=jnp.float32).astype(jnp.bfloat16)


def expert_backward(token_rows, grad_rows, gate_cols, up_cols, down_rows):
    last_dims = (((1,), (1,)), ((), ()))
    first_dims = (((0,), (0,)), ((), ()))
    gate_pre = jnp.dot(token_rows, gate_cols, preferred_element_type=jnp.float32)
    up_pre = jnp.dot(token_rows, up_cols, preferred_element_type=jnp.float32)
    gate_sig = jax.nn.sigmoid(gate_pre)
    active = gate_pre * gate_sig
    hidden = (active * up_pre).astype(jnp.bfloat16)
    grad_hidden = lax.dot_general(
        grad_rows, down_rows, last_dims, preferred_element_type=jnp.float32
    )
    grad_down = lax.dot_general(hidden, grad_rows, first_dims, preferred_element_type=jnp.float32)
    grad_gate_pre = (grad_hidden * up_pre * gate_sig * (1.0 + gate_pre * (1.0 - gate_sig))).astype(
        jnp.bfloat16
    )
    grad_up_pre = (grad_hidden * active).astype(jnp.bfloat16)
    grad_gate = lax.dot_general(
        token_rows, grad_gate_pre, first_dims, preferred_element_type=jnp.float32
    )
    grad_up = lax.dot_general(
        token_rows, grad_up_pre, first_dims, preferred_element_type=jnp.float32
    )
    grad_part = lax.dot_general(
        grad_gate_pre, gate_cols, last_dims, preferred_element_type=jnp.float32
    )
    grad_part = grad_part + lax.dot_general(
        grad_up_pre, up_cols, last_dims, preferred_element_type=jnp.float32
    )
    return (grad_gate, grad_up, grad_down, grad_part.astype(jnp.bfloat16))


def body(
    fresh_tokens,
    sent_forward,
    sent_backward,
    turn_gradient,
    saved_input,
    gain,
    ids_front,
    affinity_front,
    ids_back,
    affinity_back,
    w_gate,
    w_up,
    w_down,
    mirror_gate,
    mirror_up,
    mirror_down,
):
    section_id = lax.axis_index("section")
    last_section = lax.axis_size("section") - 1
    groups = lax.axis_size("ep") // EXPERTS
    tokens = fresh_tokens.shape[0]
    capacity = max(groups, tokens * ids_front.shape[2] * 2 // EXPERTS)
    model_width = fresh_tokens.shape[1]
    arrived = passed_along(sent_forward, "section", 1)
    returned = passed_along(sent_backward, "section", -1)
    front_in = jnp.where(section_id == 0, fresh_tokens, arrived[0])
    upstream_in = jnp.where(section_id == last_section, turn_gradient, returned[0])
    values, inverse, normed = norm_rows(front_in, gain[0])
    member, weighted = slot_tables(ids_front[0], affinity_front[0], capacity)
    packed = jnp.dot(
        member.T.astype(jnp.bfloat16), normed, preferred_element_type=jnp.float32
    ).astype(jnp.bfloat16)
    arrived_rows = to_experts(packed, groups)
    partial_value = expert_partial(
        arrived_rows.reshape(-1, model_width), w_gate[0], w_up[0], w_down[0]
    )
    totals = from_experts(partial_value.reshape(arrived_rows.shape), groups)
    mixed = values + jnp.dot(weighted, totals, precision=highest)
    forward_out = mixed.astype(jnp.bfloat16)[None]
    saved_values, saved_inverse, saved_normed = norm_rows(saved_input[0], gain[0])
    member_back, weighted_back = slot_tables(ids_back[0], affinity_back[0], capacity)
    upstream = upstream_in.astype(jnp.float32)
    packed_rows = jnp.dot(
        member_back.T.astype(jnp.bfloat16), saved_normed, preferred_element_type=jnp.float32
    ).astype(jnp.bfloat16)
    packed_grads = jnp.dot(weighted_back.T, upstream, precision=highest).astype(jnp.bfloat16)
    both_rows = to_experts(jnp.concatenate([packed_rows, packed_grads], axis=1), groups)
    flat_rows = both_rows.reshape(-1, 2 * model_width)
    grad_gate, grad_up, grad_down, grad_part = expert_backward(
        flat_rows[:, :model_width], flat_rows[:, model_width:], w_gate[0], w_up[0], w_down[0]
    )
    slot_grads = from_experts(
        grad_part.reshape(both_rows.shape[0], both_rows.shape[1], model_width), groups
    )
    grad_normed = jnp.dot(member_back, slot_grads, precision=highest)
    scaled = grad_normed * gain[0].astype(jnp.float32)
    cubed = saved_inverse * saved_inverse * saved_inverse
    grad_inputs = (
        upstream
        + saved_inverse * scaled
        - cubed * saved_values * jnp.mean(scaled * saved_values, axis=-1, keepdims=True)
    )
    out_gate = (mirror_gate[0].astype(jnp.float32) + grad_gate).astype(jnp.bfloat16)[None]
    out_up = (mirror_up[0].astype(jnp.float32) + grad_up).astype(jnp.bfloat16)[None]
    out_down = (mirror_down[0].astype(jnp.float32) + grad_down).astype(jnp.bfloat16)[None]
    return (forward_out, grad_inputs.astype(jnp.bfloat16)[None], out_gate, out_up, out_down)


def solution(mesh):
    return jax.shard_map(
        body,
        mesh=mesh,
        in_specs=(
            P("ep", None),
            P("section", "ep", None),
            P("section", "ep", None),
            P("ep", None),
            P("section", "ep", None),
            P("section", None),
            P("section", "ep", None),
            P("section", "ep", None),
            P("section", "ep", None),
            P("section", "ep", None),
            P("section", None, "ep"),
            P("section", None, "ep"),
            P("section", "ep", None),
            P("section", None, "ep"),
            P("section", None, "ep"),
            P("section", "ep", None),
        ),
        out_specs=(
            P("section", "ep", None),
            P("section", "ep", None),
            P("section", None, "ep"),
            P("section", None, "ep"),
            P("section", "ep", None),
        ),
        check_vma=False,
    )
```

profile of v0, /device:TPU:1, one launch (start us, length us, event | category | flops | bytes accessed | tf_op | source)
XLA Modules:
  0.0 95.4 jit_solution(14718165702587920896)
XLA Ops:
  0.6 4.0 %collective-permute-start = (bf16[1,16,3584]{2,1,0:T(8,128)(2,1)}, bf16[1,16,3584]{2,1,0:T(8,128)(2,1)S(1)}, u32[]{:S(2)}, u32[]{:S(2)}) collective-permute-start(bf16[1,16,3584]{2,1,0:T(8,128)(2,1)} %param.17), channel_id=1, source_target_pairs={{0,8},{8,16},{16,24},{1,9},{9,17},{17,25},{2,10},{10,18},{18,26},{... | collective-permute-start | bytes 344072 | tf_op jit(solution)/shard_map/ppermute | solution.py:15
  4.7 1.3 %collective-permute-start.1 = (bf16[1,16,3584]{2,1,0:T(8,128)(2,1)}, bf16[1,16,3584]{2,1,0:T(8,128)(2,1)S(1)}, u32[]{:S(2)}, u32[]{:S(2)}) collective-permute-start(bf16[1,16,3584]{2,1,0:T(8,128)(2,1)} %param.18), channel_id=1, source_target_pairs={{8,0},{16,8},{24,16},{9,1},{17,9},{25,17},{10,2},{18,10},{26,18},{... | collective-permute-start | bytes 344072 | tf_op jit(solution)/shard_map/ppermute | solution.py:15
  6.0 0.7 reduce_sum.113
  6.7 0.7 bitcast_divide_fusion.1
  7.4 0.7 reduce_sum.121
  8.1 0.7 bitcast_divide_fusion
  8.7 1.0 %fusion.68 = f32[16]{0:T(128)S(1)} fusion(bf16[1,16,3584]{2,1,0:T(8,128)(2,1)} %param.20), kind=kLoop, calls=%fused_computation.70 | loop fusion | flops 172016 | bytes 114752 | tf_op jit(solution)/shard_map/reduce_sum | solution.py:24
  9.8 0.8 copy.37
  10.6 0.1 eq.63
  10.7 0.8 copy.39
  11.4 0.1 eq.71
  11.5 0.8 convert_reduce_fusion.2
  12.3 0.1 fusion.85
  12.4 0.2 select_reduce_fusion.1
  12.6 0.1 reduce_sum.119
  12.7 0.1 copy.40
  12.7 0.7 bitcast_add_fusion
  13.4 0.1 fusion.86
  13.6 0.2 select_reduce_fusion.3
  13.8 0.1 reduce_sum.112
  13.8 0.1 copy.38
  13.9 0.7 bitcast_add_fusion.1
  14.6 0.1 select_reduce_fusion
  14.7 1.2 %convolution_convert_fusion.1 = bf16[64,3584]{1,0:T(8,128)(2,1)S(1)} fusion(bf16[1,16,3584]{2,1,0:T(8,128)(2,1)} %param.20, f32[16]{0:T(128)S(1)} %get-tuple-element.14, f32[3584]{0:T(1024)S(1)} %convert_reduce_fusion.2, f32[16,64]{1,0:T(8,128)S(1)} %get-tuple-element.6), kind=kOutput, calls=%fused_computation.29 | convolution fusion | flops 7799808 | bytes 591936 | tf_op jit(solution)/shard_map/dot_general | solution.py:147
  15.9 0.1 convert_reduce_fusion.1
  16.0 1.1 %fusion.65 = (f32[16]{0:T(128)S(1)}, bf16[16,3584]{1,0:T(8,128)(2,1)S(1)}) fusion(bf16[16,3584]{1,0:T(8,128)(2,1)} %param.16, bf16[1,16,3584]{2,1,0:T(8,128)(2,1)S(1)} %collective-permute-done, pred[]{:T(512)S(6)} %eq.62), kind=kLoop, calls=%fused_computation.67 | loop fusion | flops 229360 | bytes 344129 | tf_op jit(solution)/shard_map/reduce_sum | solution.py:24
  17.1 1.1 %fusion.31 = bf16[8,8,3584]{2,1,0:T(8,128)(2,1)} fusion(bf16[16,3584]{1,0:T(8,128)(2,1)S(1)} %get-tuple-element.10, f32[3584]{0:T(1024)S(1)} %convert_reduce_fusion.2, f32[16]{0:T(128)S(1)} %add_rsqrt_fusion.1, bf16[16,64]{1,0:T(8,128)(2,1)S(1)} %get-tuple-element.7), kind=kOutput, calls=%fused_computation.31 | convolution fusion | flops 7798784 | bytes 589888 | tf_op jit(solution)/shard_map/dot_general | solution.py:134
  18.2 4.7 %all-to-all-start = ((bf16[8,8,3584]{2,1,0:T(8,128)(2,1)}), bf16[8,8,3584]{2,1,0:T(8,128)(2,1)S(1)}, u32[]{:S(2)}, u32[]{:S(2)}) async-start(bf16[8,8,3584]{2,1,0:T(8,128)(2,1)} %fusion.31), calls=%async_computation | async-start | bytes 917504 | tf_op jit(solution)/shard_map/all_to_all | solution.py:47
  22.9 0.6 convolution_convert_fusion
  23.4 1.0 %maximum_bitcast_fusion = bf16[8,8,7168]{2,1,0:T(8,128)(2,1)} fusion(bf16[64,3584]{1,0:T(8,128)(2,1)S(1)} %convolution_convert_fusion, bf16[64,3584]{1,0:T(8,128)(2,1)S(1)} %convolution_convert_fusion.1), kind=kLoop, calls=%fused_computation.40 | loop fusion | flops 1835008 | bytes 1835008 | tf_op jit(solution)/shard_map/reshape;reshape | solution.py:48
  24.4 4.8 %all-to-all-done = bf16[8,8,3584]{2,1,0:T(8,128)(2,1)S(1)} async-done(((bf16[8,8,3584]{2,1,0:T(8,128)(2,1)}), bf16[8,8,3584]{2,1,0:T(8,128)(2,1)S(1)}, u32[]{:S(2)}, u32[]{:S(2)}) %all-to-all-start) | async-done | bytes 458784 | tf_op jit(solution)/shard_map/all_to_all | solution.py:47
  29.2 6.1 %all-to-all-start.2 = ((bf16[8,8,7168]{2,1,0:T(8,128)(2,1)}), bf16[8,8,7168]{2,1,0:T(8,128)(2,1)S(1)}, u32[]{:S(2)}, u32[]{:S(2)}) async-start(bf16[8,8,7168]{2,1,0:T(8,128)(2,1)} %maximum_bitcast_fusion), calls=%async_computation.2 | async-start | bytes 1835008 | tf_op jit(solution)/shard_map/all_to_all | solution.py:47
  35.4 4.5 %fusion.17 = f32[64,1024]{1,0:T(8,128)S(1)} fusion(bf16[1,3584,1024]{2,1,0:T(8,128)(2,1)} %param.26, bf16[8,8,3584]{2,1,0:T(8,128)(2,1)S(1)} %all-to-all-done), kind=kOutput, calls=%fused_computation.20 | convolution fusion | flops 469762048 | bytes 8060928 | tf_op jit(solution)/shard_map/dot_general | solution.py:67
  39.8 8.6 %fusion.32 = bf16[8,8,3584]{2,1,0:T(8,128)(2,1)} fusion(bf16[1,1024,3584]{2,1,0:T(8,128)(2,1)} %param.28, bf16[1,3584,1024]{2,1,0:T(8,128)(2,1)} %param.27, bf16[8,8,3584]{2,1,0:T(8,128)(2,1)S(1)} %all-to-all-done, f32[64,1024]{1,0:T(8,128)S(1)} %fusion.17), kind=kOutput, calls=%fused_computation.32 | convolution fusion | flops 940146688 | bytes 15859712 | tf_op jit(solution)/shard_map/dot_general | solution.py:70
  48.5 4.3 %all-to-all-start.1 = ((bf16[8,8,3584]{2,1,0:T(8,128)(2,1)}), bf16[8,8,3584]{2,1,0:T(8,128)(2,1)S(1)}, u32[]{:S(2)}, u32[]{:S(2)}) async-start(bf16[8,8,3584]{2,1,0:T(8,128)(2,1)} %fusion.32), calls=%async_computation.1 | async-start | bytes 917504 | tf_op jit(solution)/shard_map/all_to_all | solution.py:59
  52.8 4.6 %fusion.9 = f32[64,1024]{1,0:T(8,128)S(1)} fusion(bf16[1,3584,1024]{2,1,0:T(8,128)(2,1)} %param.27, bf16[64,7168]{1,0:T(8,128)(2,1)S(1)} %bitcast.122), kind=kOutput, calls=%fused_computation.12 | convolution fusion | flops 469762048 | bytes 8060928 | tf_op jit(solution)/shard_map/dot_general | solution.py:77
  57.4 5.5 %fusion.3 = f32[64,1024]{1,0:T(8,128)S(1)} fusion(bf16[1,1024,3584]{2,1,0:T(8,128)(2,1)} %param.28, bf16[64,7168]{1,0:T(8,128)(2,1)S(1)} %bitcast.123), kind=kOutput, calls=%fused_computation.6 | convolution fusion | flops 469762048 | bytes 8060928 | tf_op jit(solution)/shard_map/dot_general | solution.py:81
  63.0 1.5 %multiply_convert_fusion.2 = (bf16[64,1024]{1,0:T(8,128)(2,1)S(1)}, bf16[64,1024]{1,0:T(8,128)(2,1)S(1)}, f32[64,1024]{1,0:T(8,128)S(1)}) fusion(f32[64,1024]{1,0:T(8,128)S(1)} %fusion.3, f32[64,1024]{1,0:T(8,128)S(1)} %fusion.9, bf16[1,3584,1024]{2,1,0:T(8,128)(2,1)S(1)} %bitcast.121, bf16[64,7168]{1,0:T(8,128)(2,1)S(1)} %bitcast.124), kind=kOutput, calls=%fused_computation.59 | convolution fusion | flops 470614016 | bytes 8847360 | tf_op jit(solution)/shard_map/dot_general | solution.py:76
  64.5 0.4 slice-done.1
  64.9 2.3 %fusion.7 = f32[64,3584]{1,0:T(8,128)S(1)} fusion(bf16[64,1024]{1,0:T(8,128)(2,1)S(1)} %get-tuple-element.12, bf16[1,3584,1024]{2,1,0:T(8,128)(2,1)S(1)} %bitcast.119), kind=kOutput, calls=%fused_computation.10 | convolution fusion | flops 469762048 | bytes 8388608 | tf_op jit(solution)/shard_map/dot_general | solution.py:98
  67.3 5.2 %fusion.21 = bf16[1,1024,3584]{2,1,0:T(8,128)(2,1)} fusion(bf16[1,1024,3584]{2,1,0:T(8,128)(2,1)S(1)} %bitcast.129, bf16[64,7168]{1,0:T(8,128)(2,1)S(1)} %bitcast.125, f32[64,1024]{1,0:T(8,128)S(1)} %fusion.9, f32[64,1024]{1,0:T(8,128)S(1)} %get-tuple-element.15), kind=kOutput, calls=%fused_computation.24 | convolution fusion | flops 481165312 | bytes 15663104 | tf_op jit(solution)/shard_map/dot_general | solution.py:84
  72.5 5.1 %fusion.19 = bf16[1,3584,1024]{2,1,0:T(8,128)(2,1)} fusion(bf16[64,1024]{1,0:T(8,128)(2,1)S(1)} %get-tuple-element.11, bf16[1,3584,1024]{2,1,0:T(8,128)(2,1)S(1)} %bitcast.131, bf16[64,7168]{1,0:T(8,128)(2,1)S(1)} %bitcast.126), kind=kOutput, calls=%fused_computation.22 | convolution fusion | flops 480772096 | bytes 15269888 | tf_op jit(solution)/shard_map/dot_general | solution.py:89
  77.6 3.1 %fusion.35 = bf16[8,8,3584]{2,1,0:T(8,128)(2,1)} fusion(f32[64,3584]{1,0:T(8,128)S(1)} %fusion.7, bf16[64,1024]{1,0:T(8,128)(2,1)S(1)} %get-tuple-element.11, bf16[1,3584,1024]{2,1,0:T(8,128)(2,1)S(1)} %bitcast.121), kind=kOutput, calls=%fused_computation.33 | convolution fusion | flops 470220800 | bytes 8847360 | tf_op jit(solution)/shard_map/dot_general | solution.py:95
  80.7 4.2 %all-to-all-start.3 = ((bf16[8,8,3584]{2,1,0:T(8,128)(2,1)}), bf16[8,8,3584]{2,1,0:T(8,128)(2,1)S(1)}, u32[]{:S(2)}, u32[]{:S(2)}) async-start(bf16[8,8,3584]{2,1,0:T(8,128)(2,1)} %fusion.35), calls=%async_computation.3 | async-start | bytes 917504 | tf_op jit(solution)/shard_map/all_to_all | solution.py:59
  84.9 0.9 fusion.39
  85.9 8.3 %fusion.20 = bf16[1,3584,1024]{2,1,0:T(8,128)(2,1)} fusion(bf16[64,1024]{1,0:T(8,128)(2,1)S(1)} %get-tuple-element.12, bf16[1,3584,1024]{2,1,0:T(8,128)(2,1)} %param.30, bf16[64,7168]{1,0:T(8,128)(2,1)S(1)} %bitcast.127), kind=kOutput, calls=%fused_computation.23 | convolution fusion | flops 480772096 | bytes 15269888 | tf_op jit(solution)/shard_map/dot_general | solution.py:92
  94.2 0.4 fusion.74
  94.6 0.8 fusion.76
  (33 shorter events, 0.2 us)
Async XLA Ops:
  0.6 15.4 %collective-permute-start = (bf16[1,16,3584]{2,1,0:T(8,128)(2,1)}, bf16[1,16,3584]{2,1,0:T(8,128)(2,1)S(1)}, u32[]{:S(2)}, u32[]{:S(2)}) collective-permute-start(bf16[1,16,3584]{2,1,0:T(8,128)(2,1)} %param.17), channel_id=1, source_target_pairs={{0,8},{8,16},{16,24},{1,9},{9,17},{17,25},{2,10},{10,18},{18,26},{... | collective-permute-start | bytes 344072 | tf_op jit(solution)/shard_map/ppermute | solution.py:15
  4.7 18.2 %collective-permute-start.1 = (bf16[1,16,3584]{2,1,0:T(8,128)(2,1)}, bf16[1,16,3584]{2,1,0:T(8,128)(2,1)S(1)}, u32[]{:S(2)}, u32[]{:S(2)}) collective-permute-start(bf16[1,16,3584]{2,1,0:T(8,128)(2,1)} %param.18), channel_id=1, source_target_pairs={{8,0},{16,8},{24,16},{9,1},{17,9},{25,17},{10,2},{18,10},{26,18},{... | collective-permute-start | bytes 344072 | tf_op jit(solution)/shard_map/ppermute | solution.py:15
  18.2 11.0 %all-to-all-start = ((bf16[8,8,3584]{2,1,0:T(8,128)(2,1)}), bf16[8,8,3584]{2,1,0:T(8,128)(2,1)S(1)}, u32[]{:S(2)}, u32[]{:S(2)}) async-start(bf16[8,8,3584]{2,1,0:T(8,128)(2,1)} %fusion.31), calls=%async_computation | async-start | bytes 917504 | tf_op jit(solution)/shard_map/all_to_all | solution.py:47
  29.2 19.2 %all-to-all-start.2 = ((bf16[8,8,7168]{2,1,0:T(8,128)(2,1)}), bf16[8,8,7168]{2,1,0:T(8,128)(2,1)S(1)}, u32[]{:S(2)}, u32[]{:S(2)}) async-start(bf16[8,8,7168]{2,1,0:T(8,128)(2,1)} %maximum_bitcast_fusion), calls=%async_computation.2 | async-start | bytes 1835008 | tf_op jit(solution)/shard_map/all_to_all | solution.py:47
  48.5 32.3 %all-to-all-start.1 = ((bf16[8,8,3584]{2,1,0:T(8,128)(2,1)}), bf16[8,8,3584]{2,1,0:T(8,128)(2,1)S(1)}, u32[]{:S(2)}, u32[]{:S(2)}) async-start(bf16[8,8,3584]{2,1,0:T(8,128)(2,1)} %fusion.32), calls=%async_computation.1 | async-start | bytes 917504 | tf_op jit(solution)/shard_map/all_to_all | solution.py:59
  52.8 10.2 %slice-start.2 = ((s8[7340032]{0:T(1024)(128)(4,1)}), s8[4194304]{0:T(1024)(128)(4,1)S(1)}, s32[]{:S(2)}) async-start(s8[7340032]{0:T(1024)(128)(4,1)} %bitcast.120), calls=%async_computation.6 | async-start | bytes 8388608
  52.8 10.2 %slice-start.3 = ((s8[7340032]{0:T(1024)(128)(4,1)}), s8[3145728]{0:T(1024)(128)(4,1)S(1)}, s32[]{:S(2)}) async-start(s8[7340032]{0:T(1024)(128)(4,1)} %bitcast.120), calls=%async_computation.7 | async-start | bytes 6291456
  57.4 7.1 %slice-start = ((s8[7340032]{0:T(1024)(128)(4,1)}), s8[4194304]{0:T(1024)(128)(4,1)S(1)}, s32[]{:S(2)}) async-start(s8[7340032]{0:T(1024)(128)(4,1)} %bitcast.118), calls=%async_computation.4 | async-start | bytes 8388608
  57.4 9.8 %slice-start.4 = ((s8[7340032]{0:T(1024)(128)(4,1)}), s8[4194304]{0:T(1024)(128)(4,1)S(1)}, s32[]{:S(2)}) async-start(s8[7340032]{0:T(1024)(128)(4,1)} %bitcast.128), calls=%async_computation.8 | async-start | bytes 8388608
  63.0 1.9 %slice-start.1 = ((s8[7340032]{0:T(1024)(128)(4,1)}), s8[3145728]{0:T(1024)(128)(4,1)S(1)}, s32[]{:S(2)}) async-start(s8[7340032]{0:T(1024)(128)(4,1)} %bitcast.118), calls=%async_computation.5 | async-start | bytes 6291456
  63.0 4.2 %slice-start.5 = ((s8[7340032]{0:T(1024)(128)(4,1)}), s8[3145728]{0:T(1024)(128)(4,1)S(1)}, s32[]{:S(2)}) async-start(s8[7340032]{0:T(1024)(128)(4,1)} %bitcast.128), calls=%async_computation.9 | async-start | bytes 6291456
  64.9 7.6 %slice-start.6 = ((s8[7340032]{0:T(1024)(128)(4,1)}), s8[4194304]{0:T(1024)(128)(4,1)S(1)}, s32[]{:S(2)}) async-start(s8[7340032]{0:T(1024)(128)(4,1)} %bitcast.130), calls=%async_computation.10 | async-start | bytes 8388608
  67.3 5.2 %slice-start.7 = ((s8[7340032]{0:T(1024)(128)(4,1)}), s8[3145728]{0:T(1024)(128)(4,1)S(1)}, s32[]{:S(2)}) async-start(s8[7340032]{0:T(1024)(128)(4,1)} %bitcast.130), calls=%async_computation.11 | async-start | bytes 6291456
  80.7 13.5 %all-to-all-start.3 = ((bf16[8,8,3584]{2,1,0:T(8,128)(2,1)}), bf16[8,8,3584]{2,1,0:T(8,128)(2,1)S(1)}, u32[]{:S(2)}, u32[]{:S(2)}) async-start(bf16[8,8,3584]{2,1,0:T(8,128)(2,1)} %fusion.35), calls=%async_computation.3 | async-start | bytes 917504 | tf_op jit(solution)/shard_map/all_to_all | solution.py:59
  85.9 8.3 %copy-start = (bf16[1,16,3584]{2,1,0:T(8,128)(2,1)S(1)}, bf16[1,16,3584]{2,1,0:T(8,128)(2,1)}, u32[]{:S(2)}) copy-start(bf16[1,16,3584]{2,1,0:T(8,128)(2,1)} %param.20) | copy-start | bytes 344068
  85.9 8.7 %copy-start.1 = (bf16[16,3584]{1,0:T(8,128)(2,1)S(1)}, bf16[16,3584]{1,0:T(8,128)(2,1)}, u32[]{:S(2)}) copy-start(bf16[16,3584]{1,0:T(8,128)(2,1)} %param.19) | copy-start | bytes 344068
where the time goes:
time: 96.2 us; the launch traced here: 95.4 us
  matrix products  53 us (55%)
  starting transfers between devices  24.7 us (26%)
  other arithmetic  9.57 us (10%)
  waiting for transfers between devices  4.83 us (5%)
  local copies, waits for them, and re-layouts  2.44 us (3%)
    all_to_all x2, starting transfers between devices, to_experts(): lax.all_to_all(sending.reshape(EXPERTS * groups, capacity, row_width), 'e...  10.8 us
    dot_general x1, matrix products, expert_partial(): jnp.dot(hidden, down_rows, preferred_element_type=jnp.float32)  8.63 us
    all_to_all x2, starting transfers between devices, from_experts(): lax.all_to_all(partial_value, 'ep', split_axis=0, concat_axis=0, tiled=True)  8.54 us
    dot_general x1, matrix products, expert_backward(): lax.dot_general(token_rows, grad_up_pre, first_dims, preferred_element_ty...  8.27 us
    dot_general x1, matrix products, expert_backward(): lax.dot_general(grad_rows, down_rows, last_dims, preferred_element_type=j...  5.54 us
    ppermute x2, starting transfers between devices, passed_along(): return lax.ppermute(value, axis, pairs)  5.33 us
    dot_general x1, matrix products, expert_backward(): lax.dot_general(hidden, grad_rows, first_dims, preferred_element_type=jnp...  5.17 us
    dot_general x1, matrix products, expert_backward(): lax.dot_general(token_rows, grad_gate_pre, first_dims, preferred_element_...  5.15 us
  transfers between devices with their start and end apart: 6, of which 1 were waited for; matrix products, arithmetic and copies ran while one was open for 66% of the time, Pallas kernels for 0%

commit v1 on v0

v1 whole, which is shorter than its diff:
```python
import functools

import jax
import jax.numpy as jnp
from jax import lax
from jax.experimental import pallas as pl
from jax.experimental.pallas import tpu as pltpu
from jax.sharding import PartitionSpec as P

EXPERTS = 8
F32 = jnp.float32
BF16 = jnp.bfloat16
MIB = 1 << 20


def dot_nn(a, b):
    return jnp.dot(a, b, preferred_element_type=F32)


def dot_nt(a, b):
    return lax.dot_general(a, b, (((1,), (1,)), ((), ())), preferred_element_type=F32)


def dot_tn(a, b):
    return lax.dot_general(a, b, (((0,), (0,)), ((), ())), preferred_element_type=F32)


def norm_rows(values, gain):
    inverse = lax.rsqrt(jnp.mean(values * values, axis=-1, keepdims=True) + 1e-06)
    return inverse, (values * inverse * gain).astype(BF16)


def choice_tables(ids, capacity, groups):
    tokens = ids.shape[0]
    columns = EXPERTS * groups * capacity
    column = lax.broadcasted_iota(jnp.int32, (tokens, columns), 1)
    expert = column // (groups * capacity)
    slot = (column % capacity).astype(F32)
    named = [(ids[:, j : j + 1] == expert).astype(F32) for j in range(2)]
    row = lax.broadcasted_iota(jnp.int32, (tokens, tokens), 0)
    col = lax.broadcasted_iota(jnp.int32, (tokens, tokens), 1)
    earlier = dot_nn((col < row).astype(BF16), (named[0] + named[1]).astype(BF16))
    here = (earlier == slot).astype(F32)
    return [(n * here).astype(BF16) for n in named]


def shares_of(affinity):
    total = affinity[:, 0:1] + affinity[:, 1:2]
    return affinity[:, 0:1] / total, affinity[:, 1:2] / total


def pack_kernel(
    capacity,
    groups,
    place_ref,
    arrived_ref,
    fresh_ref,
    returned_ref,
    turn_ref,
    saved_ref,
    gain_ref,
    ids_front_ref,
    ids_back_ref,
    aff_back_ref,
    packed_ref,
    front_ref,
    upstream_ref,
):
    width = fresh_ref.shape[1]
    gain = gain_ref[...].astype(F32)
    front = jnp.where(place_ref[0] == 0, fresh_ref[...].astype(F32), arrived_ref[...].astype(F32))
    upstream = jnp.where(
        place_ref[1] == 0, turn_ref[...].astype(F32), returned_ref[...].astype(F32)
    )
    front_ref[...] = front.astype(BF16)
    upstream_ref[...] = upstream.astype(BF16)
    _, normed = norm_rows(front, gain)
    first, second = choice_tables(ids_front_ref[...], capacity, groups)
    packed_ref[:, :width] = dot_tn(first + second, normed).astype(BF16)
    _, normed = norm_rows(saved_ref[...].astype(F32), gain)
    first, second = choice_tables(ids_back_ref[...], capacity, groups)
    packed_ref[:, width : 2 * width] = dot_tn(first + second, normed).astype(BF16)
    shares = shares_of(aff_back_ref[...])
    packed_ref[:, 2 * width :] = (
        dot_tn(first, (shares[0] * upstream).astype(BF16))
        + dot_tn(second, (shares[1] * upstream).astype(BF16))
    ).astype(BF16)


def expert_kernel(
    rows_ref, gate_ref, up_ref, down_ref, parts_ref, rows_t_ref, hidden_t_ref, dgate_ref, dup_ref, both_ref, front_acc, back_acc
):
    step = pl.program_id(0)
    count = rows_ref.shape[0]
    width = gate_ref.shape[0]

    @pl.when(step == 0)
    def _():
        both_ref[:count] = rows_ref[:, :width]
        both_ref[count:] = rows_ref[:, width : 2 * width]
        rows_t_ref[...] = rows_ref[:, width : 2 * width].T
        front_acc[...] = jnp.zeros_like(front_acc)
        back_acc[...] = jnp.zeros_like(back_acc)

    both = both_ref[...]
    gate_pre = dot_nn(both, gate_ref[...])
    up_pre = dot_nn(both, up_ref[...])
    sig = jax.nn.sigmoid(gate_pre)
    active = gate_pre * sig
    hidden = (active * up_pre).astype(BF16)
    front_acc[...] += dot_nn(hidden[:count], down_ref[...])
    grad_hidden = dot_nt(rows_ref[:, 2 * width :], down_ref[...])
    back = slice(count, 2 * count)
    dgate = (grad_hidden * up_pre[back] * sig[back] * (1.0 + gate_pre[back] * (1.0 - sig[back]))).astype(BF16)
    dup = (grad_hidden * active[back]).astype(BF16)
    back_acc[...] += dot_nt(dgate, gate_ref[...]) + dot_nt(dup, up_ref[...])
    hidden_t_ref[...] = hidden[back].T
    dgate_ref[...] = dgate
    dup_ref[...] = dup

    @pl.when(step == pl.num_programs(0) - 1)
    def _():
        parts_ref[:, :width] = front_acc[...].astype(BF16)
        parts_ref[:, width:] = back_acc[...].astype(BF16)


def grads_kernel(
    rows_t_ref, hidden_t_ref, dgate_ref, dup_ref, grads_ref, mgate_ref, mup_ref, mdown_ref, ogate_ref, oup_ref, odown_ref
):
    rows_t = rows_t_ref[...]
    ogate_ref[...] = (mgate_ref[...].astype(F32) + dot_nn(rows_t, dgate_ref[...])).astype(BF16)
    oup_ref[...] = (mup_ref[...].astype(F32) + dot_nn(rows_t, dup_ref[...])).astype(BF16)
    odown_ref[...] = (mdown_ref[...].astype(F32) + dot_nn(hidden_t_ref[...], grads_ref[...])).astype(BF16)


def combine_kernel(
    capacity,
    groups,
    parts_ref,
    front_ref,
    upstream_ref,
    saved_ref,
    gain_ref,
    ids_front_ref,
    aff_front_ref,
    ids_back_ref,
    forward_ref,
    input_ref,
):
    width = front_ref.shape[1]
    first, second = choice_tables(ids_front_ref[...], capacity, groups)
    shares = shares_of(aff_front_ref[...])
    parts = parts_ref[:, :width]
    forward_ref[...] = (
        front_ref[...].astype(F32) + shares[0] * dot_nn(first, parts) + shares[1] * dot_nn(second, parts)
    ).astype(BF16)
    first, second = choice_tables(ids_back_ref[...], capacity, groups)
    gain = gain_ref[...].astype(F32)
    saved = saved_ref[...].astype(F32)
    inverse, _ = norm_rows(saved, gain)
    scaled = dot_nn(first + second, parts_ref[:, width:]) * gain
    cubed = inverse * inverse * inverse
    input_ref[...] = (
        upstream_ref[...].astype(F32)
        + inverse * scaled
        - cubed * saved * jnp.mean(scaled * saved, axis=-1, keepdims=True)
    ).astype(BF16)


def shape(dims, dtype=BF16):
    return jax.ShapeDtypeStruct(dims, dtype)


def whole(memory_space=pltpu.VMEM):
    return pl.BlockSpec(memory_space=memory_space)


def cost(flops, moved):
    return pl.CostEstimate(flops=int(flops), bytes_accessed=int(moved), transcendentals=0)


def exchanged(rows):
    return lax.all_to_all(rows, "ep", split_axis=0, concat_axis=0, tiled=True)


def ring(value, by):
    size = lax.axis_size("section")
    return lax.ppermute(value, "section", [(i, (i + by) % size) for i in range(size)])


def body(
    fresh_tokens,
    sent_forward,
    sent_backward,
    turn_gradient,
    saved_input,
    gain,
    ids_front,
    affinity_front,
    ids_back,
    affinity_back,
    w_gate,
    w_up,
    w_down,
    mirror_gate,
    mirror_up,
    mirror_down,
):
    peers = lax.axis_size("ep")
    groups = peers // EXPERTS
    tokens, width = fresh_tokens.shape
    capacity = max(groups, tokens * ids_front.shape[2] * 2 // EXPERTS)
    count = peers * capacity
    units = w_gate.shape[2]
    section_id = lax.axis_index("section")
    place = jnp.stack([section_id, lax.axis_size("section") - 1 - section_id]).astype(jnp.int32)
    returned = ring(sent_backward, -1)
    arrived = ring(sent_forward, 1)
    packed, front, upstream = pl.pallas_call(
        functools.partial(pack_kernel, capacity, groups),
        out_shape=(shape((count, 3 * width)), shape((tokens, width)), shape((tokens, width))),
        in_specs=[whole(pltpu.SMEM)] + [whole()] * 9,
        out_specs=(whole(),) * 3,
        compiler_params=pltpu.CompilerParams(vmem_limit_bytes=24 * MIB),
        cost_estimate=cost(2 * count * tokens * width * 4, 5 * count * width),
        name="pack_rows",
    )(
        place,
        arrived[0],
        fresh_tokens,
        returned[0],
        turn_gradient,
        saved_input[0],
        gain,
        ids_front[0],
        ids_back[0],
        affinity_back[0],
    )
    rows = exchanged(packed.reshape(peers, capacity, 3 * width)).reshape(count, 3 * width)
    chunk = min(256, units)
    parts, rows_t, hidden_t, dgate, dup = pl.pallas_call(
        expert_kernel,
        grid=(units // chunk,),
        out_shape=(
            shape((count, 2 * width)),
            shape((width, count)),
            shape((units, count)),
            shape((count, units)),
            shape((count, units)),
        ),
        in_specs=[
            pl.BlockSpec((count, 3 * width), lambda i: (0, 0)),
            pl.BlockSpec((width, chunk), lambda i: (0, i)),
            pl.BlockSpec((width, chunk), lambda i: (0, i)),
            pl.BlockSpec((chunk, width), lambda i: (i, 0)),
        ],
        out_specs=(
            pl.BlockSpec((count, 2 * width), lambda i: (0, 0)),
            pl.BlockSpec((width, count), lambda i: (0, 0)),
            pl.BlockSpec((chunk, count), lambda i: (i, 0)),
            pl.BlockSpec((count, chunk), lambda i: (0, i)),
            pl.BlockSpec((count, chunk), lambda i: (0, i)),
        ),
        scratch_shapes=[
            pltpu.VMEM((2 * count, width), BF16),
            pltpu.VMEM((count, width), F32),
            pltpu.VMEM((count, width), F32),
        ],
        compiler_params=pltpu.CompilerParams(vmem_limit_bytes=(28 if count <= 128 else 60) * MIB),
        cost_estimate=cost(2 * count * width * units * 8, 6 * width * units),
        name="expert_rows",
    )(rows, w_gate[0], w_up[0], w_down[0])
    back = exchanged(parts.reshape(peers, capacity, 2 * width)).reshape(count, 2 * width)
    steps = 8
    wide, deep = width // steps, units // steps
    grads = rows[:, 2 * width :]
    gate_spec = pl.BlockSpec((wide, units), lambda i: (i, 0))
    down_spec = pl.BlockSpec((deep, width), lambda i: (i, 0))
    out_gate, out_up, out_down = pl.pallas_call(
        grads_kernel,
        grid=(steps,),
        out_shape=(shape((width, units)), shape((width, units)), shape((units, width))),
        in_specs=[
            pl.BlockSpec((wide, count), lambda i: (i, 0)),
            pl.BlockSpec((deep, count), lambda i: (i, 0)),
            pl.BlockSpec((count, units), lambda i: (0, 0)),
            pl.BlockSpec((count, units), lambda i: (0, 0)),
            pl.BlockSpec((count, width), lambda i: (0, 2)),
            gate_spec,
            gate_spec,
            down_spec,
        ],
        out_specs=(gate_spec, gate_spec, down_spec),
        compiler_params=pltpu.CompilerParams(vmem_limit_bytes=24 * MIB),
        cost_estimate=cost(2 * count * width * units * 3, 12 * width * units),
        name="weight_grads",
    )(rows_t, hidden_t, dgate, dup, rows, mirror_gate[0], mirror_up[0], mirror_down[0])
    forward_out, grad_input = pl.pallas_call(
        functools.partial(combine_kernel, capacity, groups),
        out_shape=(shape((tokens, width)), shape((tokens, width))),
        in_specs=[whole()] * 8,
        out_specs=(whole(),) * 2,
        compiler_params=pltpu.CompilerParams(vmem_limit_bytes=24 * MIB),
        cost_estimate=cost(2 * count * tokens * width * 3, 4 * count * width),
        name="combine_rows",
    )(
        back,
        front,
        upstream,
        saved_input[0],
        gain,
        ids_front[0],
        affinity_front[0],
        ids_back[0],
    )
    return (forward_out[None], grad_input[None], out_gate[None], out_up[None], out_down[None])


def solution(mesh):
    return jax.shard_map(
        body,
        mesh=mesh,
        in_specs=(
            P("ep", None),
            P("section", "ep", None),
            P("section", "ep", None),
            P("ep", None),
            P("section", "ep", None),
            P("section", None),
            P("section", "ep", None),
            P("section", "ep", None),
            P("section", "ep", None),
            P("section", "ep", None),
            P("section", None, "ep"),
            P("section", None, "ep"),
            P("section", "ep", None),
            P("section", None, "ep"),
            P("section", None, "ep"),
            P("section", "ep", None),
        ),
        out_specs=(
            P("section", "ep", None),
            P("section", "ep", None),
            P("section", None, "ep"),
            P("section", None, "ep"),
            P("section", "ep", None),
        ),
        check_vma=False,
    )
```

time: 96.2 us -> 95.2 us (0.990)
  matrix products: 53 us -> 0 us
  Pallas kernels: 0 us -> 30.5 us
  local copies, waits for them, and re-layouts: 2.44 us -> 29.3 us
  blocking collectives: 0 us -> 22.8 us
  starting transfers between devices: 24.7 us -> 8.46 us
  other arithmetic: 9.57 us -> 0.07 us
  waiting for transfers between devices: 4.83 us -> 2.69 us
    dot_general x15 -> x0, matrix products: 53 us -> none  [the longest x1 8.63 us: expert_partial(): jnp.dot(hidden, down_rows, preferred_element_type=jnp.float32)]
    pallas_call x0 -> x4, Pallas kernels: none -> 30.5 us  [the longest x1 17.7 us: body(): pl.pallas_call(expert_kernel, grid=(units // chunk,), out_shape=(shape((c...]
    unnamed x22 -> x42, local copies, waits for them, and re-layouts: 1.94 us -> 26.9 us
    all_to_all x0 -> x1, blocking collectives: none -> 22.8 us  [exchanged(): return lax.all_to_all(rows, 'ep', split_axis=0, concat_axis=0, tiled=True)]
    all_to_all x4 -> x1, starting transfers between devices: 19.3 us -> 4.19 us  [exchanged(): return lax.all_to_all(rows, 'ep', split_axis=0, concat_axis=0, tiled=True)]
    all_to_all x4 -> x1, waiting for transfers between devices: 4.83 us -> 0.01 us  [exchanged(): return lax.all_to_all(rows, 'ep', split_axis=0, concat_axis=0, tiled=True)]
    reduce_sum x8 -> x0, other arithmetic: 4.02 us -> none  [the longest x2 2.1 us: norm_rows(): jnp.mean(values * values, axis=-1, keepdims=True) + 1e-06]
    ppermute x2, waiting for transfers between devices: 0.01 us -> 2.68 us  [ring(): lax.ppermute(value, 'section', [(i, (i + by) % size) for i in range(size)])]
  transfers between devices with their start and end apart: 6 -> 3, of which waited for: 1 -> 2; matrix products, arithmetic and copies ran while one was open for 66% -> 3% of each run, Pallas kernels for 0% -> 10%
where the time goes in v1:
time: 95.2 us; the launch traced here: 94.4 us
  Pallas kernels  30.5 us (32%)
  local copies, waits for them, and re-layouts  29.3 us (31%)
  blocking collectives  22.8 us (24%)
  starting transfers between devices  8.46 us (9%)
  waiting for transfers between devices  2.69 us (3%)
    unnamed x42, local copies, waits for them, and re-layouts  26.9 us
    all_to_all x1, blocking collectives, exchanged(): return lax.all_to_all(rows, 'ep', split_axis=0, concat_axis=0, tiled=True)  22.8 us
    pallas_call x1, Pallas kernels, body(): pl.pallas_call(expert_kernel, grid=(units // chunk,), out_shape=(shape((c...  17.7 us
    pallas_call x1, Pallas kernels, body(): pl.pallas_call(grads_kernel, grid=(steps,), out_shape=(shape((width, unit...  9.79 us
    ppermute x2, starting transfers between devices, ring(): lax.ppermute(value, 'section', [(i, (i + by) % size) for i in range(size)])  4.27 us
    all_to_all x1, starting transfers between devices, exchanged(): return lax.all_to_all(rows, 'ep', split_axis=0, concat_axis=0, tiled=True)  4.19 us
    ppermute x2, waiting for transfers between devices, ring(): lax.ppermute(value, 'section', [(i, (i + by) % size) for i in range(size)])  2.68 us
  transfers between devices with their start and end apart: 3, of which 2 were waited for; matrix products, arithmetic and copies ran while one was open for 3% of the time, Pallas kernels for 10%

profile of v1, /device:TPU:1, one launch (start us, length us, event | category | flops | bytes accessed | tf_op | source)
XLA Modules:
  0.0 94.4 jit_solution(2252621161839699583)
XLA Ops:
  0.6 2.2 %collective-permute-start = (bf16[1,16,3584]{2,1,0:T(8,128)(2,1)}, bf16[1,16,3584]{2,1,0:T(8,128)(2,1)S(1)}, u32[]{:S(2)}, u32[]{:S(2)}) collective-permute-start(bf16[1,16,3584]{2,1,0:T(8,128)(2,1)} %param.17), channel_id=1, source_target_pairs={{0,8},{8,16},{16,24},{24,0},{1,9},{9,17},{17,25},{25,1},{2,10},{10... | collective-permute-start | bytes 344072 | tf_op jit(solution)/shard_map/ppermute | solution.py:188
  2.8 2.1 %collective-permute-start.1 = (bf16[1,16,3584]{2,1,0:T(8,128)(2,1)}, bf16[1,16,3584]{2,1,0:T(8,128)(2,1)S(1)}, u32[]{:S(2)}, u32[]{:S(2)}) collective-permute-start(bf16[1,16,3584]{2,1,0:T(8,128)(2,1)} %param.18), channel_id=1, source_target_pairs={{0,24},{8,0},{16,8},{24,16},{1,25},{9,1},{17,9},{25,17},{2,26},{10... | collective-permute-start | bytes 344072 | tf_op jit(solution)/shard_map/ppermute | solution.py:188
  4.9 0.8 copy.21.ids_front_ref
  5.7 0.8 copy.22.ids_back_ref
  6.4 0.8 copy.23.aff_back_ref
  7.2 0.1 pad_add_fusion.place_ref
  7.2 0.7 collective-permute-done
  7.9 2.0 %collective-permute-done.1 = bf16[1,16,3584]{2,1,0:T(8,128)(2,1)S(1)} collective-permute-done((bf16[1,16,3584]{2,1,0:T(8,128)(2,1)}, bf16[1,16,3584]{2,1,0:T(8,128)(2,1)S(1)}, u32[]{:S(2)}, u32[]{:S(2)}) %collective-permute-start.1) | collective-permute-done | bytes 114720 | tf_op jit(solution)/shard_map/ppermute | solution.py:188
  9.9 0.0 copy-start.6
  9.9 0.9 copy-done.6
  10.8 0.0 copy-start.16
  10.8 0.9 copy-done.16
  11.7 0.0 copy-start.17
  11.7 0.9 copy-done.17
  12.6 0.0 copy-start.18
  12.6 0.7 copy-done.18
  13.3 1.6 %pack_rows.1 = (bf16[64,10752]{1,0:T(8,128)(2,1)S(1)}, bf16[16,3584]{1,0:T(8,128)(2,1)S(1)}, bf16[16,3584]{1,0:T(8,128)(2,1)S(1)}) custom-call(s32[2]{0:T(128)S(1)} %pad_add_fusion.place_ref, bf16[16,3584]{1,0:T(8,128)(2,1)S(1)} %bitcast.36, bf16[16,3584]{1,0:T(8,128)(2,1)S(1)} %copy-done.16, bf16[16,3584]{1,0:T(8,128)(2,1)S(1)} %bitcast.37, ...), custom_call_target="tpu_custom_call" | custom-call | flops 29360128 | bytes 1146880 | tf_op jit(solution)/shard_map/pack_rows/pallas_call | solution.py:219
  14.9 0.0 copy-start.12
  14.9 0.0 copy-start.14
  14.9 22.8 %all_to_all.10 = bf16[8,8,10752]{2,1,0:T(8,128)(2,1)S(1)} all-to-all(bf16[8,8,10752]{2,1,0:T(8,128)(2,1)S(1)} %bitcast.33), channel_id=1, replica_groups=mesh['section'=4,'ep'=8] {'ep'}, dimensions={0} | all-to-all | bytes 2752512 | tf_op jit(solution)/shard_map/all_to_all | solution.py:183
  37.7 0.0 copy-done.12
  37.7 0.0 copy-done.14
  37.7 0.0 copy-start
  37.7 3.1 %copy-done = bf16[1,3584,1024]{2,1,0:T(8,128)(2,1)S(1)} copy-done((bf16[1,3584,1024]{2,1,0:T(8,128)(2,1)S(1)}, bf16[1,3584,1024]{2,1,0:T(8,128)(2,1)}, u32[]{:S(2)}) %copy-start) | copy-done | bytes 7340056
  40.8 0.0 copy-start.1
  40.8 3.1 %copy-done.1 = bf16[1,3584,1024]{2,1,0:T(8,128)(2,1)S(1)} copy-done((bf16[1,3584,1024]{2,1,0:T(8,128)(2,1)S(1)}, bf16[1,3584,1024]{2,1,0:T(8,128)(2,1)}, u32[]{:S(2)}) %copy-start.1) | copy-done | bytes 7340056
  43.9 0.0 copy-start.2
  43.9 3.1 %copy-done.2 = bf16[1,1024,3584]{2,1,0:T(8,128)(2,1)S(1)} copy-done((bf16[1,1024,3584]{2,1,0:T(8,128)(2,1)S(1)}, bf16[1,1024,3584]{2,1,0:T(8,128)(2,1)}, u32[]{:S(2)}) %copy-start.2) | copy-done | bytes 7340056
  47.0 0.0 copy-start.20
  47.0 17.7 %expert_rows.1 = (bf16[64,7168]{1,0:T(8,128)(2,1)}, bf16[3584,64]{1,0:T(8,128)(2,1)S(1)}, bf16[1024,64]{1,0:T(8,128)(2,1)S(1)}, bf16[64,1024]{1,0:T(8,128)(2,1)S(1)}, bf16[64,1024]{1,0:T(8,128)(2,1)S(1)}) custom-call(bf16[64,10752]{1,0:T(8,128)(2,1)S(1)} %bitcast.24, bf16[3584,1024]{1,0:T(8,128)(2,1)S(1)} %bitcast.26, bf16[3584,1024]{1,0:T(8,128)(2,1)S(1)} %bitcast.27, ...), custom_call_target="tpu_custom_call" | custom-call | flops 3758096384 | bytes 22020096 | tf_op jit(solution)/shard_map/expert_rows/pallas_call | solution.py:241
  64.7 0.7 copy-done.8
  65.4 0.7 copy-done.10
  66.0 4.2 %all-to-all-start.1 = ((bf16[8,8,7168]{2,1,0:T(8,128)(2,1)}), bf16[8,8,7168]{2,1,0:T(8,128)(2,1)S(1)}, u32[]{:S(2)}, u32[]{:S(2)}) async-start(bf16[8,8,7168]{2,1,0:T(8,128)(2,1)} %bitcast.13), calls=%async_computation.1 | async-start | bytes 1835008 | tf_op jit(solution)/shard_map/all_to_all | solution.py:183
  70.2 0.0 copy-done.20
  70.2 0.1 copy.25.aff_front_ref
  70.3 3.1 %copy-done.3 = bf16[1,3584,1024]{2,1,0:T(8,128)(2,1)S(1)} copy-done((bf16[1,3584,1024]{2,1,0:T(8,128)(2,1)S(1)}, bf16[1,3584,1024]{2,1,0:T(8,128)(2,1)}, u32[]{:S(2)}) %copy-start.3) | copy-done | bytes 7340056
  73.4 3.1 %copy-done.4 = bf16[1,3584,1024]{2,1,0:T(8,128)(2,1)S(1)} copy-done((bf16[1,3584,1024]{2,1,0:T(8,128)(2,1)S(1)}, bf16[1,3584,1024]{2,1,0:T(8,128)(2,1)}, u32[]{:S(2)}) %copy-start.4) | copy-done | bytes 7340056
  76.5 3.1 %copy-done.5 = bf16[1,1024,3584]{2,1,0:T(8,128)(2,1)S(1)} copy-done((bf16[1,1024,3584]{2,1,0:T(8,128)(2,1)S(1)}, bf16[1,1024,3584]{2,1,0:T(8,128)(2,1)}, u32[]{:S(2)}) %copy-start.5) | copy-done | bytes 7340056
  79.6 0.9 %copy-done.9 = bf16[1024,64]{1,0:T(8,128)(2,1)S(1)} copy-done((bf16[1024,64]{1,0:T(8,128)(2,1)S(1)}, bf16[1024,64]{1,0:T(8,128)(2,1)}, u32[]{:S(2)}) %copy-start.9) | copy-done | bytes 131096
  80.5 0.9 copy-done.11
  81.4 9.8 %weight_grads.1 = (bf16[3584,1024]{1,0:T(8,128)(2,1)}, bf16[3584,1024]{1,0:T(8,128)(2,1)}, bf16[1024,3584]{1,0:T(8,128)(2,1)}) custom-call(bf16[3584,64]{1,0:T(8,128)(2,1)S(1)} %get-tuple-element.24.rows_t_ref, bf16[1024,64]{1,0:T(8,128)(2,1)S(1)} %copy-done.9, bf16[64,1024]{1,0:T(8,128)(2,1)S(1)} %get-tuple-element.26.dgate_ref, ...), custom_call_target="tpu_custom_call" | custom-call | flops 1409286144 | bytes 44040192 | tf_op jit(solution)/shard_map/weight_grads/pallas_call | solution.py:279
  91.2 0.0 all-to-all-done.1
  91.2 0.0 copy-done.7
  91.2 0.0 copy-done.19
  91.2 0.0 copy-start.13
  91.2 0.9 copy-done.13
  92.1 0.9 copy-done.15
  93.0 1.4 %combine_rows.1 = (bf16[16,3584]{1,0:T(8,128)(2,1)}, bf16[16,3584]{1,0:T(8,128)(2,1)}) custom-call(bf16[64,7168]{1,0:T(8,128)(2,1)S(1)} %bitcast.32, bf16[16,3584]{1,0:T(8,128)(2,1)S(1)} %copy-done.13, bf16[16,3584]{1,0:T(8,128)(2,1)S(1)} %copy-done.15, bf16[16,3584]{1,0:T(8,128)(2,1)S(1)} %bitcast.35, bf16[1,3584]{1,0:T(2,128)(2,1)S(1)} %copy-done.19, ...), custom_call_target="tpu_custom_call" | custom-call | flops 22020096 | bytes 917504 | tf_op jit(solution)/shard_map/combine_rows/pallas_call | solution.py:298
  (10 shorter events, 0.0 us)
Async XLA Ops:
  0.6 7.3 %collective-permute-start = (bf16[1,16,3584]{2,1,0:T(8,128)(2,1)}, bf16[1,16,3584]{2,1,0:T(8,128)(2,1)S(1)}, u32[]{:S(2)}, u32[]{:S(2)}) collective-permute-start(bf16[1,16,3584]{2,1,0:T(8,128)(2,1)} %param.17), channel_id=1, source_target_pairs={{0,8},{8,16},{16,24},{24,0},{1,9},{9,17},{17,25},{25,1},{2,10},{10... | collective-permute-start | bytes 344072 | tf_op jit(solution)/shard_map/ppermute | solution.py:188
  2.8 7.1 %collective-permute-start.1 = (bf16[1,16,3584]{2,1,0:T(8,128)(2,1)}, bf16[1,16,3584]{2,1,0:T(8,128)(2,1)S(1)}, u32[]{:S(2)}, u32[]{:S(2)}) collective-permute-start(bf16[1,16,3584]{2,1,0:T(8,128)(2,1)} %param.18), channel_id=1, source_target_pairs={{0,24},{8,0},{16,8},{24,16},{1,25},{9,1},{17,9},{25,17},{2,26},{10... | collective-permute-start | bytes 344072 | tf_op jit(solution)/shard_map/ppermute | solution.py:188
  9.9 0.9 copy-start.6
  10.8 0.9 copy-start.16
  11.7 0.9 copy-start.17
  12.6 0.7 copy-start.18
  14.9 22.8 %copy-start.12 = (bf16[16,3584]{1,0:T(8,128)(2,1)}, bf16[16,3584]{1,0:T(8,128)(2,1)S(1)}, u32[]{:S(2)}) copy-start(bf16[16,3584]{1,0:T(8,128)(2,1)S(1)} %get-tuple-element.20.front_ref) | copy-start | bytes 344068
  14.9 22.8 %copy-start.14 = (bf16[16,3584]{1,0:T(8,128)(2,1)}, bf16[16,3584]{1,0:T(8,128)(2,1)S(1)}, u32[]{:S(2)}) copy-start(bf16[16,3584]{1,0:T(8,128)(2,1)S(1)} %get-tuple-element.21.upstream_ref) | copy-start | bytes 344068
  37.7 3.1 %copy-start = (bf16[1,3584,1024]{2,1,0:T(8,128)(2,1)S(1)}, bf16[1,3584,1024]{2,1,0:T(8,128)(2,1)}, u32[]{:S(2)}) copy-start(bf16[1,3584,1024]{2,1,0:T(8,128)(2,1)} %param.26) | copy-start | bytes 22020100
  40.8 3.1 %copy-start.1 = (bf16[1,3584,1024]{2,1,0:T(8,128)(2,1)S(1)}, bf16[1,3584,1024]{2,1,0:T(8,128)(2,1)}, u32[]{:S(2)}) copy-start(bf16[1,3584,1024]{2,1,0:T(8,128)(2,1)} %param.27) | copy-start | bytes 22020100
  43.9 3.1 %copy-start.2 = (bf16[1,1024,3584]{2,1,0:T(8,128)(2,1)S(1)}, bf16[1,1024,3584]{2,1,0:T(8,128)(2,1)}, u32[]{:S(2)}) copy-start(bf16[1,1024,3584]{2,1,0:T(8,128)(2,1)} %param.28) | copy-start | bytes 22020100
  47.0 23.3 %copy-start.20 = (f32[1,16,2]{1,2,0:T(2,128)S(1)}, f32[1,16,2]{1,2,0:T(2,128)}, u32[]{:S(2)}) copy-start(f32[1,16,2]{1,2,0:T(2,128)} %param.23) | copy-start | bytes 388
  64.7 0.7 copy-start.8
  65.4 0.7 copy-start.10
  66.0 25.2 %all-to-all-start.1 = ((bf16[8,8,7168]{2,1,0:T(8,128)(2,1)}), bf16[8,8,7168]{2,1,0:T(8,128)(2,1)S(1)}, u32[]{:S(2)}, u32[]{:S(2)}) async-start(bf16[8,8,7168]{2,1,0:T(8,128)(2,1)} %bitcast.13), calls=%async_computation.1 | async-start | bytes 1835008 | tf_op jit(solution)/shard_map/all_to_all | solution.py:183
  70.3 3.1 %copy-start.3 = (bf16[1,3584,1024]{2,1,0:T(8,128)(2,1)S(1)}, bf16[1,3584,1024]{2,1,0:T(8,128)(2,1)}, u32[]{:S(2)}) copy-start(bf16[1,3584,1024]{2,1,0:T(8,128)(2,1)} %param.29) | copy-start | bytes 22020100
  73.4 3.1 %copy-start.4 = (bf16[1,3584,1024]{2,1,0:T(8,128)(2,1)S(1)}, bf16[1,3584,1024]{2,1,0:T(8,128)(2,1)}, u32[]{:S(2)}) copy-start(bf16[1,3584,1024]{2,1,0:T(8,128)(2,1)} %param.30) | copy-start | bytes 22020100
  76.5 3.1 %copy-start.5 = (bf16[1,1024,3584]{2,1,0:T(8,128)(2,1)S(1)}, bf16[1,1024,3584]{2,1,0:T(8,128)(2,1)}, u32[]{:S(2)}) copy-start(bf16[1,1024,3584]{2,1,0:T(8,128)(2,1)} %param.31) | copy-start | bytes 22020100
  79.6 0.9 %copy-start.9 = (bf16[1024,64]{1,0:T(8,128)(2,1)S(1)}, bf16[1024,64]{1,0:T(8,128)(2,1)}, u32[]{:S(2)}) copy-start(bf16[1024,64]{1,0:T(8,128)(2,1)} %copy-done.8) | copy-start | bytes 393220
  80.5 0.9 copy-start.11
  81.4 9.8 %copy-start.7 = (bf16[1,16,3584]{2,1,0:T(8,128)(2,1)S(1)}, bf16[1,16,3584]{2,1,0:T(8,128)(2,1)}, u32[]{:S(2)}) copy-start(bf16[1,16,3584]{2,1,0:T(8,128)(2,1)} %param.20) | copy-start | bytes 344068
  81.4 9.8 %copy-start.19 = (bf16[1,3584]{1,0:T(2,128)(2,1)S(1)}, bf16[1,3584]{1,0:T(2,128)(2,1)}, u32[]{:S(2)}) copy-start(bf16[1,3584]{1,0:T(2,128)(2,1)} %gain_ref.3) | copy-start | bytes 21508
  91.2 0.9 copy-start.13
  92.1 0.9 copy-start.15

commit v2 on v1

v2 whole, which is shorter than its diff:
```python
import functools

import jax
import jax.numpy as jnp
from jax import lax
from jax.experimental import pallas as pl
from jax.experimental.pallas import tpu as pltpu
from jax.sharding import PartitionSpec as P

EXPERTS = 8
F32 = jnp.float32
BF16 = jnp.bfloat16
MIB = 1 << 20


def dot_nn(a, b):
    return jnp.dot(a, b, preferred_element_type=F32)


def dot_nt(a, b):
    return lax.dot_general(a, b, (((1,), (1,)), ((), ())), preferred_element_type=F32)


def dot_tn(a, b):
    return lax.dot_general(a, b, (((0,), (0,)), ((), ())), preferred_element_type=F32)


def norm_rows(values, gain):
    inverse = lax.rsqrt(jnp.mean(values * values, axis=-1, keepdims=True) + 1e-06)
    return inverse, (values * inverse * gain).astype(BF16)


def choice_tables(ids, capacity, groups, flip):
    tokens = ids.shape[1]
    count = EXPERTS * groups * capacity
    row = lax.broadcasted_iota(jnp.int32, (count, tokens), 0)
    expert = ((row // capacity) ^ flip) // groups
    slot = (row % capacity).astype(F32)
    named = [(ids[j : j + 1, :] == expert).astype(F32) for j in range(2)]
    one = lax.broadcasted_iota(jnp.int32, (tokens, tokens), 0)
    other = lax.broadcasted_iota(jnp.int32, (tokens, tokens), 1)
    earlier = dot_nn((named[0] + named[1]).astype(BF16), (one < other).astype(BF16))
    here = (earlier == slot).astype(F32)
    return [n * here for n in named]


def shares_of(affinity):
    total = affinity[0:1, :] + affinity[1:2, :]
    return affinity[0:1, :] / total, affinity[1:2, :] / total


def as_column(row):
    size = row.shape[1]
    one = lax.broadcasted_iota(jnp.int32, (size, size), 0)
    other = lax.broadcasted_iota(jnp.int32, (size, size), 1)
    return jnp.sum(jnp.where(one == other, row, 0.0), axis=1, keepdims=True)


def early_kernel(
    capacity,
    groups,
    place_ref,
    fresh_hbm,
    turn_hbm,
    saved_hbm,
    gain_hbm,
    ids_front_hbm,
    aff_front_hbm,
    ids_back_hbm,
    aff_back_hbm,
    fresh_ref,
    turn_ref,
    saved_ref,
    gain_ref,
    rows_ref,
    front_table_ref,
    front_picks_ref,
    front_shares_ref,
    back_table_ref,
    back_picks_ref,
    slot_shares_ref,
    ids_front_ref,
    aff_front_ref,
    ids_back_ref,
    aff_back_ref,
    sems,
):
    pairs = (
        (ids_front_hbm, ids_front_ref),
        (aff_front_hbm, aff_front_ref),
        (ids_back_hbm, ids_back_ref),
        (aff_back_hbm, aff_back_ref),
        (saved_hbm, saved_ref),
        (gain_hbm, gain_ref),
        (fresh_hbm, fresh_ref),
        (turn_hbm, turn_ref),
    )
    copies = [pltpu.make_async_copy(*pair, sems.at[i]) for i, pair in enumerate(pairs)]
    for copy in copies:
        copy.start()
    for copy in copies[:4]:
        copy.wait()
    flip = place_ref[2]
    first, second = choice_tables(ids_front_ref[...], capacity, groups, flip)
    front_table_ref[...] = (first + second).astype(BF16)
    front_picks_ref[0] = first.T.astype(BF16)
    front_picks_ref[1] = second.T.astype(BF16)
    share = shares_of(aff_front_ref[...])
    front_shares_ref[0] = as_column(share[0])
    front_shares_ref[1] = as_column(share[1])
    first, second = choice_tables(ids_back_ref[...], capacity, groups, flip)
    both = first + second
    back_table_ref[...] = both.astype(BF16)
    back_picks_ref[...] = both.T.astype(BF16)
    share = shares_of(aff_back_ref[...])
    slot_shares_ref[...] = jnp.sum(first * share[0] + second * share[1], axis=1, keepdims=True)
    copies[4].wait()
    copies[5].wait()
    _, normed = norm_rows(saved_ref[...].astype(F32), gain_ref[...].astype(F32))
    rows_ref[...] = dot_nn(back_table_ref[...], normed).astype(BF16)
    copies[6].wait()
    copies[7].wait()


def pack_kernel(
    place_ref,
    arrived_ref,
    fresh_ref,
    returned_ref,
    turn_ref,
    gain_ref,
    rows_ref,
    front_table_ref,
    back_table_ref,
    slot_shares_ref,
    front_ref,
    upstream_ref,
    *packed_refs,
):
    width = fresh_ref.shape[1]
    front = jnp.where(place_ref[0] == 0, fresh_ref[...].astype(F32), arrived_ref[...].astype(F32))
    upstream = jnp.where(place_ref[1] == 0, turn_ref[...].astype(F32), returned_ref[...].astype(F32))
    front_ref[...] = front.astype(BF16)
    upstream_ref[...] = upstream.astype(BF16)
    _, normed = norm_rows(front, gain_ref[...].astype(F32))
    front_rows = dot_nn(front_table_ref[...], normed).astype(BF16)
    grad_rows = (slot_shares_ref[...] * dot_nn(back_table_ref[...], upstream.astype(BF16))).astype(BF16)
    back_rows = rows_ref[...]
    for i, packed_ref in enumerate(packed_refs):
        at = slice(i * packed_ref.shape[0], (i + 1) * packed_ref.shape[0])
        packed_ref[:, :width] = front_rows[at]
        packed_ref[:, width : 2 * width] = back_rows[at]
        packed_ref[:, 2 * width :] = grad_rows[at]


def load_kernel(amount, *refs):
    after, sources, targets, sems = refs[0], refs[1 : 1 + amount], refs[1 + amount : 1 + 2 * amount], refs[-1]
    del after
    copies = [pltpu.make_async_copy(a, b, sems.at[i]) for i, (a, b) in enumerate(zip(sources, targets))]
    for copy in copies:
        copy.start()
    for copy in copies:
        copy.wait()


def expert_kernel(
    chunk,
    tile,
    pieces,
    gate_ref,
    up_ref,
    down_ref,
    *refs,
):
    rows_refs, refs = refs[:pieces], refs[pieces:]
    grads_ref, rows_t_ref, hidden_t_ref, dgate_ref, dup_ref = refs[:5]
    parts_refs = refs[5 : 5 + pieces]
    both_ref, grads_t_ref, dgate_t_ref, dup_t_ref, front_ref = refs[5 + pieces :]
    width, units = gate_ref.shape
    count = grads_ref.shape[0]
    each = count // pieces
    rows = jnp.concatenate([ref[...] for ref in rows_refs], axis=0)
    both_ref[:count] = rows[:, :width]
    both_ref[count:] = rows[:, width : 2 * width]
    grads_ref[...] = rows[:, 2 * width :]
    rows_t_ref[...] = rows[:, width : 2 * width].T
    grads_t_ref[...] = rows[:, 2 * width :].T
    for i in range(units // chunk):
        at = slice(i * chunk, (i + 1) * chunk)
        gate_pre = dot_nn(both_ref[...], gate_ref[:, at])
        up_pre = dot_nn(both_ref[...], up_ref[:, at])
        sig = jax.nn.sigmoid(gate_pre)
        active = gate_pre * sig
        hidden = active * up_pre
        front_ref[:, at] = hidden[:count].astype(BF16)
        hidden_t_ref[at, :] = hidden[count:].T.astype(BF16)
        grad_hidden = dot_nn(down_ref[at, :], grads_t_ref[...]).T
        slope = up_pre[count:] * sig[count:] * (1.0 + gate_pre[count:] * (1.0 - sig[count:]))
        dgate = grad_hidden * slope
        dup = grad_hidden * active[count:]
        dgate_ref[:, at] = dgate.astype(BF16)
        dup_ref[:, at] = dup.astype(BF16)
        dgate_t_ref[at, :] = dgate.T.astype(BF16)
        dup_t_ref[at, :] = dup.T.astype(BF16)
    for j in range(width // tile):
        at = slice(j * tile, (j + 1) * tile)
        back = dot_nn(gate_ref[at, :], dgate_t_ref[...]) + dot_nn(up_ref[at, :], dup_t_ref[...])
        back = back.T.astype(BF16)
        front = dot_nn(front_ref[...], down_ref[:, at]).astype(BF16)
        for i, parts_ref in enumerate(parts_refs):
            own = slice(i * each, (i + 1) * each)
            parts_ref[:, at] = front[own]
            parts_ref[:, width + j * tile : width + (j + 1) * tile] = back[own]


def grads_kernel(
    wide,
    deep,
    rows_t_ref,
    hidden_t_ref,
    dgate_ref,
    dup_ref,
    grads_ref,
    mgate_ref,
    mup_ref,
    mdown_ref,
    ogate_ref,
    oup_ref,
    odown_ref,
):
    at = pl.ds(pl.multiple_of(pl.program_id(0) * wide, 16), wide)
    rows_t = rows_t_ref[at, :]
    ogate_ref[...] = (mgate_ref[at, :].astype(F32) + dot_nn(rows_t, dgate_ref[...])).astype(BF16)
    oup_ref[...] = (mup_ref[at, :].astype(F32) + dot_nn(rows_t, dup_ref[...])).astype(BF16)
    at = pl.ds(pl.multiple_of(pl.program_id(0) * deep, 16), deep)
    odown_ref[...] = (mdown_ref[at, :].astype(F32) + dot_nn(hidden_t_ref[at, :], grads_ref[...])).astype(BF16)


def combine_kernel(
    front_ref,
    upstream_ref,
    saved_ref,
    gain_ref,
    front_picks_ref,
    front_shares_ref,
    back_picks_ref,
    *refs,
):
    forward_ref, input_ref = refs[-2:]
    width = front_ref.shape[1]
    both = jnp.concatenate([ref[...] for ref in refs[:-2]], axis=0)
    parts = both[:, :width]
    forward_ref[...] = (
        front_ref[...].astype(F32)
        + front_shares_ref[0] * dot_nn(front_picks_ref[0], parts)
        + front_shares_ref[1] * dot_nn(front_picks_ref[1], parts)
    ).astype(BF16)
    gain = gain_ref[...].astype(F32)
    saved = saved_ref[...].astype(F32)
    inverse, _ = norm_rows(saved, gain)
    scaled = dot_nn(back_picks_ref[...], both[:, width:]) * gain
    cubed = inverse * inverse * inverse
    input_ref[...] = (
        upstream_ref[...].astype(F32)
        + inverse * scaled
        - cubed * saved * jnp.mean(scaled * saved, axis=-1, keepdims=True)
    ).astype(BF16)


def shape(dims, dtype=BF16):
    return jax.ShapeDtypeStruct(dims, dtype)


def held(dims, dtype=BF16):
    return pltpu.VMEM(dims, dtype)


def whole(memory_space=pltpu.VMEM):
    return pl.BlockSpec(memory_space=memory_space)


def cost(flops, moved):
    return pl.CostEstimate(flops=int(flops), bytes_accessed=int(moved), transcendentals=0)


def in_hbm(value):
    return pltpu.with_memory_space_constraint(value, pltpu.HBM)


def loaded(after, *arrays):
    amount = len(arrays)
    return pl.pallas_call(
        functools.partial(load_kernel, amount),
        out_shape=tuple(held(a.shape) for a in arrays),
        in_specs=[whole(pl.ANY)] * (1 + amount),
        out_specs=(whole(),) * amount,
        scratch_shapes=[pltpu.SemaphoreType.DMA((amount,))],
        compiler_params=pltpu.CompilerParams(vmem_limit_bytes=MIB),
        cost_estimate=cost(0, 2 * sum(a.size for a in arrays)),
        name="load_weights",
    )(after, *(in_hbm(a) for a in arrays))


def exchanged(pieces):
    if len(pieces) == 1:
        peers = lax.axis_size("ep")
        rows = pieces[0].reshape(peers, -1, pieces[0].shape[-1])
        return (lax.all_to_all(rows, "ep", split_axis=0, concat_axis=0, tiled=True).reshape(pieces[0].shape),)
    peers = range(len(pieces))
    return (pieces[0],) + tuple(lax.ppermute(pieces[i], "ep", [(j, j ^ i) for j in peers]) for i in peers[1:])


def ring(value, by):
    size = lax.axis_size("section")
    return lax.ppermute(value, "section", [(i, (i + by) % size) for i in range(size)])


def body(
    fresh_tokens,
    sent_forward,
    sent_backward,
    turn_gradient,
    saved_input,
    gain,
    ids_front,
    affinity_front,
    ids_back,
    affinity_back,
    w_gate,
    w_up,
    w_down,
    mirror_gate,
    mirror_up,
    mirror_down,
):
    peers = lax.axis_size("ep")
    groups = peers // EXPERTS
    tokens, width = fresh_tokens.shape
    capacity = max(groups, tokens * ids_front.shape[2] * 2 // EXPERTS)
    count = peers * capacity
    units = w_gate.shape[2]
    section_id = lax.axis_index("section")
    pieces = peers if peers <= 8 else 1
    flip = lax.axis_index("ep") if pieces > 1 else jnp.int32(0)
    place = jnp.stack([section_id, lax.axis_size("section") - 1 - section_id, flip]).astype(jnp.int32)
    returned = ring(sent_backward, -1)
    arrived = ring(sent_forward, 1)
    early = pl.pallas_call(
        functools.partial(early_kernel, capacity, groups),
        out_shape=(held((tokens, width)),) * 3
        + (
            held((1, width)),
            held((count, width)),
            held((count, tokens)),
            held((2, tokens, count)),
            held((2, tokens, 1), F32),
            held((count, tokens)),
            held((tokens, count)),
            held((count, 1), F32),
        ),
        in_specs=[whole(pltpu.SMEM)] + [whole(pl.ANY)] * 8,
        out_specs=(whole(),) * 11,
        scratch_shapes=[pltpu.VMEM((2, tokens), t) for t in (jnp.int32, F32, jnp.int32, F32)]
        + [pltpu.SemaphoreType.DMA((8,))],
        compiler_params=pltpu.CompilerParams(vmem_limit_bytes=4 * MIB),
        cost_estimate=cost(2 * count * tokens * width, 2 * count * width),
        name="early_rows",
    )(
        place,
        *(in_hbm(v) for v in (fresh_tokens, turn_gradient, saved_input[0], gain)),
        *(in_hbm(v[0].T) for v in (ids_front, affinity_front, ids_back, affinity_back)),
    )
    fresh, turn, saved, gain_row, back_rows = early[:5]
    front_table, front_picks, front_shares, back_table, back_picks, slot_shares = early[5:]
    front, upstream, *packed = pl.pallas_call(
        pack_kernel,
        out_shape=(held((tokens, width)),) * 2 + (shape((count // pieces, 3 * width)),) * pieces,
        in_specs=[whole(pltpu.SMEM)] + [whole()] * 9,
        out_specs=(whole(),) * (2 + pieces),
        compiler_params=pltpu.CompilerParams(vmem_limit_bytes=6 * MIB),
        cost_estimate=cost(2 * count * tokens * width * 4, 5 * count * width),
        name="pack_rows",
    )(
        place,
        arrived[0],
        fresh,
        returned[0],
        turn,
        gain_row,
        back_rows,
        front_table,
        back_table,
        slot_shares,
    )
    rows = exchanged(packed)
    (w_gate,) = loaded(packed[0], w_gate[0])
    chunk, tile = min(256, units), width // 7
    grads, rows_t, hidden_t, dgate, dup, *parts = pl.pallas_call(
        functools.partial(expert_kernel, chunk, tile, pieces),
        out_shape=(
            held((count, width)),
            held((width, count)),
            held((units, count)),
            held((count, units)),
            held((count, units)),
        )
        + (shape((count // pieces, 2 * width)),) * pieces,
        in_specs=[whole()] * (3 + pieces),
        out_specs=(whole(),) * (5 + pieces),
        scratch_shapes=[
            pltpu.VMEM((2 * count, width), BF16),
            pltpu.VMEM((width, count), BF16),
            pltpu.VMEM((units, count), BF16),
            pltpu.VMEM((units, count), BF16),
            pltpu.VMEM((count, units), BF16),
        ],
        compiler_params=pltpu.CompilerParams(vmem_limit_bytes=(6 if count <= 128 else 32) * MIB),
        cost_estimate=cost(2 * count * width * units * 8, 6 * width * units),
        name="expert_rows",
    )(w_gate, w_up[0], w_down[0], *rows)
    back = exchanged(parts)
    steps = 8
    wide, deep = width // steps, units // steps
    gate_spec = pl.BlockSpec((wide, units), lambda i: (i, 0))
    down_spec = pl.BlockSpec((deep, width), lambda i: (i, 0))
    out_gate, out_up, out_down = pl.pallas_call(
        functools.partial(grads_kernel, wide, deep),
        grid=(steps,),
        out_shape=(shape((width, units)), shape((width, units)), shape((units, width))),
        in_specs=[whole()] * 8,
        out_specs=(gate_spec, gate_spec, down_spec),
        compiler_params=pltpu.CompilerParams(vmem_limit_bytes=8 * MIB),
        cost_estimate=cost(2 * count * width * units * 3, 12 * width * units),
        name="weight_grads",
    )(rows_t, hidden_t, dgate, dup, grads, mirror_gate[0], mirror_up[0], mirror_down[0])
    forward_out, grad_input = pl.pallas_call(
        combine_kernel,
        out_shape=(shape((tokens, width)), shape((tokens, width))),
        in_specs=[whole()] * (7 + pieces),
        out_specs=(whole(),) * 2,
        compiler_params=pltpu.CompilerParams(vmem_limit_bytes=6 * MIB),
        cost_estimate=cost(2 * count * tokens * width * 3, 4 * count * width),
        name="combine_rows",
    )(front, upstream, saved, gain_row, front_picks, front_shares, back_picks, *back)
    return (forward_out[None], grad_input[None], out_gate[None], out_up[None], out_down[None])


def solution(mesh):
    return jax.shard_map(
        body,
        mesh=mesh,
        in_specs=(
            P("ep", None),
            P("section", "ep", None),
            P("section", "ep", None),
            P("ep", None),
            P("section", "ep", None),
            P("section", None),
            P("section", "ep", None),
            P("section", "ep", None),
            P("section", "ep", None),
            P("section", "ep", None),
            P("section", None, "ep"),
            P("section", None, "ep"),
            P("section", "ep", None),
            P("section", None, "ep"),
            P("section", None, "ep"),
            P("section", "ep", None),
        ),
        out_specs=(
            P("section", "ep", None),
            P("section", "ep", None),
            P("section", None, "ep"),
            P("section", None, "ep"),
            P("section", "ep", None),
        ),
        check_vma=False,
    )
```

time: 95.2 us -> 60.7 us (0.64)
  local copies, waits for them, and re-layouts: 29.3 us -> 0.04 us
  blocking collectives: 22.8 us -> 0 us
  starting transfers between devices: 8.46 us -> 23.1 us
  waiting for transfers between devices: 2.69 us -> 9.53 us
  Pallas kernels: 30.5 us -> 27 us
    unnamed x42 -> x16, local copies, waits for them, and re-layouts: 26.9 us -> 0.04 us
    all_to_all x1 -> x0, blocking collectives: 22.8 us -> none  [exchanged(): return lax.all_to_all(rows, 'ep', split_axis=0, concat_axis=0, tiled=True)]
    ppermute x0 -> x14, starting transfers between devices: none -> 18.8 us  [exchanged(): lax.ppermute(pieces[i], 'ep', [(j, j ^ i) for j in peers])]
    ppermute x0 -> x14, waiting for transfers between devices: none -> 6.58 us  [exchanged(): lax.ppermute(pieces[i], 'ep', [(j, j ^ i) for j in peers])]
    all_to_all x1 -> x0, starting transfers between devices: 4.19 us -> none  [exchanged(): return lax.all_to_all(rows, 'ep', split_axis=0, concat_axis=0, tiled=True)]
    pallas_call x4 -> x6, Pallas kernels: 30.5 us -> 27 us  [the longest x1 9.8 us: body(): pl.pallas_call(functools.partial(grads_kernel, wide, deep), grid=(steps,)...]
    squeeze x4 -> x0, local copies, waits for them, and re-layouts: 2.35 us -> none  [the longest x1 0.75 us: body(): ids_front[0]]
  transfers between devices with their start and end apart: 3 -> 16, of which waited for: 2 -> 4; matrix products, arithmetic and copies ran while one was open for 3% -> 0% of each run, Pallas kernels for 10% -> 25%
where the time goes in v2:
time: 60.7 us; the launch traced here: 60.5 us
  Pallas kernels  27 us (44%)
  starting transfers between devices  23.1 us (38%)
  waiting for transfers between devices  9.53 us (16%)
  between operations  0.79 us (1%)
    ppermute x14, starting transfers between devices, exchanged(): lax.ppermute(pieces[i], 'ep', [(j, j ^ i) for j in peers])  18.8 us
    pallas_call x1, Pallas kernels, body(): pl.pallas_call(functools.partial(grads_kernel, wide, deep), grid=(steps,)...  9.8 us
    pallas_call x1, Pallas kernels, body(): pl.pallas_call(functools.partial(expert_kernel, chunk, tile, pieces), out...  9.74 us
    ppermute x14, waiting for transfers between devices, exchanged(): lax.ppermute(pieces[i], 'ep', [(j, j ^ i) for j in peers])  6.58 us
    ppermute x2, starting transfers between devices, ring(): lax.ppermute(value, 'section', [(i, (i + by) % size) for i in range(size)])  4.27 us
    pallas_call x1, Pallas kernels, loaded(): pl.pallas_call(functools.partial(load_kernel, amount), out_shape=tuple((h...  3.24 us
    ppermute x2, waiting for transfers between devices, ring(): lax.ppermute(value, 'section', [(i, (i + by) % size) for i in range(size)])  2.95 us
    pallas_call x1, Pallas kernels, body(): pl.pallas_call(functools.partial(early_kernel, capacity, groups), out_sha...  1.99 us
  transfers between devices with their start and end apart: 16, of which 4 were waited for; matrix products, arithmetic and copies ran while one was open for 0% of the time, Pallas kernels for 25%

profile of v2, /device:TPU:1, one launch (start us, length us, event | category | flops | bytes accessed | tf_op | source)
XLA Modules:
  0.0 60.5 jit_solution(14368497062435704377)
XLA Ops:
  0.6 2.2 %collective-permute-start = (bf16[1,16,3584]{2,1,0:T(8,128)(2,1)}, bf16[1,16,3584]{2,1,0:T(8,128)(2,1)S(1)}, u32[]{:S(2)}, u32[]{:S(2)}) collective-permute-start(bf16[1,16,3584]{2,1,0:T(8,128)(2,1)} %param.17), channel_id=1, source_target_pairs={{0,8},{8,16},{16,24},{24,0},{1,9},{9,17},{17,25},{25,1},{2,10},{10... | collective-permute-start | bytes 344072 | tf_op jit(solution)/shard_map/ppermute | solution.py:315
  2.8 2.1 %collective-permute-start.1 = (bf16[1,16,3584]{2,1,0:T(8,128)(2,1)}, bf16[1,16,3584]{2,1,0:T(8,128)(2,1)S(1)}, u32[]{:S(2)}, u32[]{:S(2)}) collective-permute-start(bf16[1,16,3584]{2,1,0:T(8,128)(2,1)} %param.18), channel_id=1, source_target_pairs={{0,24},{8,0},{16,8},{24,16},{1,25},{9,1},{17,9},{25,17},{2,26},{10... | collective-permute-start | bytes 344072 | tf_op jit(solution)/shard_map/ppermute | solution.py:315
  4.9 0.1 pad_add_fusion.place_ref
  5.0 2.0 %early_rows.1 = (bf16[16,3584]{1,0:T(8,128)(2,1)S(1)}, bf16[16,3584]{1,0:T(8,128)(2,1)S(1)}, bf16[16,3584]{1,0:T(8,128)(2,1)S(1)}, bf16[1,3584]{1,0:T(2,128)(2,1...) custom-call(s32[3]{0:T(128)S(1)} %pad_add_fusion.place_ref, ...), custom_call_target="tpu_custom_call" | custom-call | flops 7340032 | bytes 458752 | tf_op jit(solution)/shard_map/early_rows/pallas_call | solution.py:348
  7.0 0.9 %collective-permute-done = bf16[1,16,3584]{2,1,0:T(8,128)(2,1)S(1)} collective-permute-done((bf16[1,16,3584]{2,1,0:T(8,128)(2,1)}, bf16[1,16,3584]{2,1,0:T(8,128)(2,1)S(1)}, u32[]{:S(2)}, u32[]{:S(2)}) %collective-permute-start) | collective-permute-done | bytes 114720 | tf_op jit(solution)/shard_map/ppermute | solution.py:315
  7.9 2.0 %collective-permute-done.1 = bf16[1,16,3584]{2,1,0:T(8,128)(2,1)S(1)} collective-permute-done((bf16[1,16,3584]{2,1,0:T(8,128)(2,1)}, bf16[1,16,3584]{2,1,0:T(8,128)(2,1)S(1)}, u32[]{:S(2)}, u32[]{:S(2)}) %collective-permute-start.1) | collective-permute-done | bytes 114720 | tf_op jit(solution)/shard_map/ppermute | solution.py:315
  9.9 1.1 %pack_rows.1 = (bf16[16,3584]{1,0:T(8,128)(2,1)S(1)}, bf16[16,3584]{1,0:T(8,128)(2,1)S(1)}, bf16[8,10752]{1,0:T(8,128)(2,1)S(1)}, bf16[8,10752]{1,0:T(8,128)(2,1...) custom-call(s32[3]{0:T(128)S(1)} %pad_add_fusion.place_ref, ...), custom_call_target="tpu_custom_call" | custom-call | flops 29360128 | bytes 1146880 | tf_op jit(solution)/shard_map/pack_rows/pallas_call | solution.py:375
  11.0 1.2 %collective-permute-start.2 = (bf16[8,10752]{1,0:T(8,128)(2,1)S(1)}, bf16[8,10752]{1,0:T(8,128)(2,1)S(1)}, u32[]{:S(2)}, u32[]{:S(2)}) collective-permute-start(bf16[8,10752]{1,0:T(8,128)(2,1)S(1)} %get-tuple-element.58), channel_id=1, source_target_pairs={{0,1},{1,0},{2,3},{3,2},{4,5},{5,4},{6,7},{7,6},{8,9},{9,8},{10,11... | collective-permute-start | bytes 516104 | tf_op jit(solution)/shard_map/ppermute | solution.py:310
  12.2 1.2 %collective-permute-start.3 = (bf16[8,10752]{1,0:T(8,128)(2,1)S(1)}, bf16[8,10752]{1,0:T(8,128)(2,1)S(1)}, u32[]{:S(2)}, u32[]{:S(2)}) collective-permute-start(bf16[8,10752]{1,0:T(8,128)(2,1)S(1)} %get-tuple-element.59), channel_id=1, source_target_pairs={{0,2},{1,3},{2,0},{3,1},{4,6},{5,7},{6,4},{7,5},{8,10},{9,11},{10,... | collective-permute-start | bytes 516104 | tf_op jit(solution)/shard_map/ppermute | solution.py:310
  13.4 0.5 collective-permute-start.4
  13.9 1.2 %collective-permute-start.5 = (bf16[8,10752]{1,0:T(8,128)(2,1)S(1)}, bf16[8,10752]{1,0:T(8,128)(2,1)S(1)}, u32[]{:S(2)}, u32[]{:S(2)}) collective-permute-start(bf16[8,10752]{1,0:T(8,128)(2,1)S(1)} %get-tuple-element.61), channel_id=1, source_target_pairs={{0,4},{1,5},{2,6},{3,7},{4,0},{5,1},{6,2},{7,3},{8,12},{9,13},{10,... | collective-permute-start | bytes 516104 | tf_op jit(solution)/shard_map/ppermute | solution.py:310
  15.1 0.6 collective-permute-start.6
  15.7 0.0 collective-permute-done.2.refs_1_
  15.7 2.2 %collective-permute-start.7 = (bf16[8,10752]{1,0:T(8,128)(2,1)S(1)}, bf16[8,10752]{1,0:T(8,128)(2,1)S(1)}, u32[]{:S(2)}, u32[]{:S(2)}) collective-permute-start(bf16[8,10752]{1,0:T(8,128)(2,1)S(1)} %get-tuple-element.63), channel_id=1, source_target_pairs={{0,6},{1,7},{2,4},{3,5},{4,2},{5,3},{6,0},{7,1},{8,14},{9,15},{10,... | collective-permute-start | bytes 516104 | tf_op jit(solution)/shard_map/ppermute | solution.py:310
  17.9 0.3 collective-permute-done.3.refs_2_
  18.1 3.4 %collective-permute-start.8 = (bf16[8,10752]{1,0:T(8,128)(2,1)S(1)}, bf16[8,10752]{1,0:T(8,128)(2,1)S(1)}, u32[]{:S(2)}, u32[]{:S(2)}) collective-permute-start(bf16[8,10752]{1,0:T(8,128)(2,1)S(1)} %get-tuple-element.64), channel_id=1, source_target_pairs={{0,7},{1,6},{2,5},{3,4},{4,3},{5,2},{6,1},{7,0},{8,15},{9,14},{10,... | collective-permute-start | bytes 516104 | tf_op jit(solution)/shard_map/ppermute | solution.py:310
  21.5 3.2 %load_weights.1.gate_ref = bf16[3584,1024]{1,0:T(8,128)(2,1)S(1)} custom-call(bf16[8,10752]{1,0:T(8,128)(2,1)S(1)} %get-tuple-element.57.refs_0_, bf16[3584,1024]{1,0:T(8,128)(2,1)} %bitcast.42), custom_call_target="tpu_custom_call" | custom-call | bytes 7340032 | tf_op jit(solution)/shard_map/load_weights/pallas_call | solution.py:292
  24.8 0.0 collective-permute-done.4.refs_3_
  24.8 0.0 collective-permute-done.5.refs_4_
  24.8 6.3 %collective-permute-done.6.refs_5_ = bf16[8,10752]{1,0:T(8,128)(2,1)S(1)} collective-permute-done((bf16[8,10752]{1,0:T(8,128)(2,1)S(1)}, bf16[8,10752]{1,0:T(8,128)(2,1)S(1)}, u32[]{:S(2)}, u32[]{:S(2)}) %collective-permute-start.6) | collective-permute-done | bytes 172064 | tf_op jit(solution)/shard_map/ppermute | solution.py:310
  31.1 0.0 collective-permute-done.7.refs_6_
  31.1 0.0 collective-permute-done.8.refs_7_
  31.1 0.0 slice-done
  31.1 0.0 slice-done.1
  31.1 0.0 copy-done
  31.1 0.0 slice-start.3
  31.1 0.0 slice-start.5
  31.1 0.0 copy-start.1
  31.1 9.7 %expert_rows.1 = (bf16[64,3584]{1,0:T(8,128)(2,1)S(1)}, bf16[3584,64]{1,0:T(8,128)(2,1)S(1)}, bf16[1024,64]{1,0:T(8,128)(2,1)S(1)}, bf16[64,1024]{1,0:T(8,128)(2...) custom-call(bf16[3584,1024]{1,0:T(8,128)(2,1)S(1)} %load_weights.1.g, ...), custom_call_target="tpu_custom_call" | custom-call | flops 3758096384 | bytes 22020096 | tf_op jit(solution)/shard_map/expert_rows/pallas_call | solution.py:398
  40.9 0.2 collective-permute-start.9
  41.1 1.2 %collective-permute-start.10 = (bf16[8,7168]{1,0:T(8,128)(2,1)S(1)}, bf16[8,7168]{1,0:T(8,128)(2,1)S(1)}, u32[]{:S(2)}, u32[]{:S(2)}) collective-permute-start(bf16[8,7168]{1,0:T(8,128)(2,1)S(1)} %get-tuple-element.67), channel_id=1, source_target_pairs={{0,2},{1,3},{2,0},{3,1},{4,6},{5,7},{6,4},{7,5},{8,10},{9,11},{10,... | collective-permute-start | bytes 344072 | tf_op jit(solution)/shard_map/ppermute | solution.py:310
  42.3 0.8 %collective-permute-start.11 = (bf16[8,7168]{1,0:T(8,128)(2,1)S(1)}, bf16[8,7168]{1,0:T(8,128)(2,1)S(1)}, u32[]{:S(2)}, u32[]{:S(2)}) collective-permute-start(bf16[8,7168]{1,0:T(8,128)(2,1)S(1)} %get-tuple-element.68), channel_id=1, source_target_pairs={{0,3},{1,2},{2,1},{3,0},{4,7},{5,6},{6,5},{7,4},{8,11},{9,10},{10,... | collective-permute-start | bytes 344072 | tf_op jit(solution)/shard_map/ppermute | solution.py:310
  43.1 1.2 %collective-permute-start.12 = (bf16[8,7168]{1,0:T(8,128)(2,1)S(1)}, bf16[8,7168]{1,0:T(8,128)(2,1)S(1)}, u32[]{:S(2)}, u32[]{:S(2)}) collective-permute-start(bf16[8,7168]{1,0:T(8,128)(2,1)S(1)} %get-tuple-element.69), channel_id=1, source_target_pairs={{0,4},{1,5},{2,6},{3,7},{4,0},{5,1},{6,2},{7,3},{8,12},{9,13},{10,... | collective-permute-start | bytes 344072 | tf_op jit(solution)/shard_map/ppermute | solution.py:310
  44.3 0.3 collective-permute-start.13
  44.6 0.0 collective-permute-done.9.refs_1_
  44.6 2.1 %collective-permute-start.14 = (bf16[8,7168]{1,0:T(8,128)(2,1)S(1)}, bf16[8,7168]{1,0:T(8,128)(2,1)S(1)}, u32[]{:S(2)}, u32[]{:S(2)}) collective-permute-start(bf16[8,7168]{1,0:T(8,128)(2,1)S(1)} %get-tuple-element.71), channel_id=1, source_target_pairs={{0,6},{1,7},{2,4},{3,5},{4,2},{5,3},{6,0},{7,1},{8,14},{9,15},{10,... | collective-permute-start | bytes 344072 | tf_op jit(solution)/shard_map/ppermute | solution.py:310
  46.7 0.0 collective-permute-done.10.refs_2_
  46.7 2.8 %collective-permute-start.15 = (bf16[8,7168]{1,0:T(8,128)(2,1)S(1)}, bf16[8,7168]{1,0:T(8,128)(2,1)S(1)}, u32[]{:S(2)}, u32[]{:S(2)}) collective-permute-start(bf16[8,7168]{1,0:T(8,128)(2,1)S(1)} %get-tuple-element.72), channel_id=1, source_target_pairs={{0,7},{1,6},{2,5},{3,4},{4,3},{5,2},{6,1},{7,0},{8,15},{9,14},{10,... | collective-permute-start | bytes 344072 | tf_op jit(solution)/shard_map/ppermute | solution.py:310
  49.5 0.0 slice-done.2
  49.5 0.0 slice-done.5
  49.5 0.0 copy-done.1
  49.6 9.8 %weight_grads.1 = (bf16[3584,1024]{1,0:T(8,128)(2,1)}, bf16[3584,1024]{1,0:T(8,128)(2,1)}, bf16[1024,3584]{1,0:T(8,128)(2,1)}) custom-call(bf16[3584,64]{1,0:T(8,128)(2,1)S(1)} %get-tuple-element.75.rows_t_ref, bf16[1024,64]{1,0:T(8,128)(2,1)S(1)} %get-tuple-element.76.hidden_t_ref, bf16[64,1024]{1,0:T(8,128)(2,1)S(1)} %get-tuple-element.77.dgate_ref, ...), custom_call_target="tpu_custom_call" | custom-call | flops 1409286144 | bytes 44040192 | tf_op jit(solution)/shard_map/weight_grads/pallas_call | solution.py:426
  59.4 0.0 collective-permute-done.11.refs_3_
  59.4 0.0 collective-permute-done.12.refs_4_
  59.4 0.0 collective-permute-done.13.refs_5_
  59.4 0.0 collective-permute-done.14.refs_6_
  59.4 0.0 collective-permute-done.15.refs_7_
  59.4 1.1 %combine_rows.1 = (bf16[16,3584]{1,0:T(8,128)(2,1)}, bf16[16,3584]{1,0:T(8,128)(2,1)}) custom-call(bf16[16,3584]{1,0:T(8,128)(2,1)S(1)} %get-tuple-element.51.front_ref, bf16[16,3584]{1,0:T(8,128)(2,1)S(1)} %get-tuple-element.52.upstream_ref, bf16[16,3584]{1,0:T(8,128)(2,1)S(1)} %get-tuple-element.53.saved_ref, ...), custom_call_target="tpu_custom_call" | custom-call | flops 22020096 | bytes 917504 | tf_op jit(solution)/shard_map/combine_rows/pallas_call | solution.py:436
  (10 shorter events, 0.0 us)
Async XLA Ops:
  0.6 7.3 %collective-permute-start = (bf16[1,16,3584]{2,1,0:T(8,128)(2,1)}, bf16[1,16,3584]{2,1,0:T(8,128)(2,1)S(1)}, u32[]{:S(2)}, u32[]{:S(2)}) collective-permute-start(bf16[1,16,3584]{2,1,0:T(8,128)(2,1)} %param.17), channel_id=1, source_target_pairs={{0,8},{8,16},{16,24},{24,0},{1,9},{9,17},{17,25},{25,1},{2,10},{10... | collective-permute-start | bytes 344072 | tf_op jit(solution)/shard_map/ppermute | solution.py:315
  2.8 7.1 %collective-permute-start.1 = (bf16[1,16,3584]{2,1,0:T(8,128)(2,1)}, bf16[1,16,3584]{2,1,0:T(8,128)(2,1)S(1)}, u32[]{:S(2)}, u32[]{:S(2)}) collective-permute-start(bf16[1,16,3584]{2,1,0:T(8,128)(2,1)} %param.18), channel_id=1, source_target_pairs={{0,24},{8,0},{16,8},{24,16},{1,25},{9,1},{17,9},{25,17},{2,26},{10... | collective-permute-start | bytes 344072 | tf_op jit(solution)/shard_map/ppermute | solution.py:315
  9.9 21.1 %slice-start = ((s8[7340032]{0:T(1024)(128)(4,1)}), s8[4194304]{0:T(1024)(128)(4,1)S(1)}, s32[]{:S(2)}) async-start(s8[7340032]{0:T(1024)(128)(4,1)} %bitcast.29), calls=%async_computation | async-start | bytes 8388608
  11.0 4.7 %collective-permute-start.2 = (bf16[8,10752]{1,0:T(8,128)(2,1)S(1)}, bf16[8,10752]{1,0:T(8,128)(2,1)S(1)}, u32[]{:S(2)}, u32[]{:S(2)}) collective-permute-start(bf16[8,10752]{1,0:T(8,128)(2,1)S(1)} %get-tuple-element.58), channel_id=1, source_target_pairs={{0,1},{1,0},{2,3},{3,2},{4,5},{5,4},{6,7},{7,6},{8,9},{9,8},{10,11... | collective-permute-start | bytes 516104 | tf_op jit(solution)/shard_map/ppermute | solution.py:310
  12.2 6.0 %collective-permute-start.3 = (bf16[8,10752]{1,0:T(8,128)(2,1)S(1)}, bf16[8,10752]{1,0:T(8,128)(2,1)S(1)}, u32[]{:S(2)}, u32[]{:S(2)}) collective-permute-start(bf16[8,10752]{1,0:T(8,128)(2,1)S(1)} %get-tuple-element.59), channel_id=1, source_target_pairs={{0,2},{1,3},{2,0},{3,1},{4,6},{5,7},{6,4},{7,5},{8,10},{9,11},{10,... | collective-permute-start | bytes 516104 | tf_op jit(solution)/shard_map/ppermute | solution.py:310
  13.4 11.3 %collective-permute-start.4 = (bf16[8,10752]{1,0:T(8,128)(2,1)S(1)}, bf16[8,10752]{1,0:T(8,128)(2,1)S(1)}, u32[]{:S(2)}, u32[]{:S(2)}) collective-permute-start(bf16[8,10752]{1,0:T(8,128)(2,1)S(1)} %get-tuple-element.60), channel_id=1, source_target_pairs={{0,3},{1,2},{2,1},{3,0},{4,7},{5,6},{6,5},{7,4},{8,11},{9,10},{10,... | collective-permute-start | bytes 516104 | tf_op jit(solution)/shard_map/ppermute | solution.py:310
  13.9 10.9 %collective-permute-start.5 = (bf16[8,10752]{1,0:T(8,128)(2,1)S(1)}, bf16[8,10752]{1,0:T(8,128)(2,1)S(1)}, u32[]{:S(2)}, u32[]{:S(2)}) collective-permute-start(bf16[8,10752]{1,0:T(8,128)(2,1)S(1)} %get-tuple-element.61), channel_id=1, source_target_pairs={{0,4},{1,5},{2,6},{3,7},{4,0},{5,1},{6,2},{7,3},{8,12},{9,13},{10,... | collective-permute-start | bytes 516104 | tf_op jit(solution)/shard_map/ppermute | solution.py:310
  15.1 15.9 %collective-permute-start.6 = (bf16[8,10752]{1,0:T(8,128)(2,1)S(1)}, bf16[8,10752]{1,0:T(8,128)(2,1)S(1)}, u32[]{:S(2)}, u32[]{:S(2)}) collective-permute-start(bf16[8,10752]{1,0:T(8,128)(2,1)S(1)} %get-tuple-element.62), channel_id=1, source_target_pairs={{0,5},{1,4},{2,7},{3,6},{4,1},{5,0},{6,3},{7,2},{8,13},{9,12},{10,... | collective-permute-start | bytes 516104 | tf_op jit(solution)/shard_map/ppermute | solution.py:310
  15.7 15.4 %collective-permute-start.7 = (bf16[8,10752]{1,0:T(8,128)(2,1)S(1)}, bf16[8,10752]{1,0:T(8,128)(2,1)S(1)}, u32[]{:S(2)}, u32[]{:S(2)}) collective-permute-start(bf16[8,10752]{1,0:T(8,128)(2,1)S(1)} %get-tuple-element.63), channel_id=1, source_target_pairs={{0,6},{1,7},{2,4},{3,5},{4,2},{5,3},{6,0},{7,1},{8,14},{9,15},{10,... | collective-permute-start | bytes 516104 | tf_op jit(solution)/shard_map/ppermute | solution.py:310
  18.1 12.9 %collective-permute-start.8 = (bf16[8,10752]{1,0:T(8,128)(2,1)S(1)}, bf16[8,10752]{1,0:T(8,128)(2,1)S(1)}, u32[]{:S(2)}, u32[]{:S(2)}) collective-permute-start(bf16[8,10752]{1,0:T(8,128)(2,1)S(1)} %get-tuple-element.64), channel_id=1, source_target_pairs={{0,7},{1,6},{2,5},{3,4},{4,3},{5,2},{6,1},{7,0},{8,15},{9,14},{10,... | collective-permute-start | bytes 516104 | tf_op jit(solution)/shard_map/ppermute | solution.py:310
  21.5 9.6 %slice-start.1 = ((s8[7340032]{0:T(1024)(128)(4,1)}), s8[3145728]{0:T(1024)(128)(4,1)S(1)}, s32[]{:S(2)}) async-start(s8[7340032]{0:T(1024)(128)(4,1)} %bitcast.29), calls=%async_computation.1 | async-start | bytes 6291456
  21.5 9.6 %copy-start = (bf16[1,1024,3584]{2,1,0:T(8,128)(2,1)S(1)}, bf16[1,1024,3584]{2,1,0:T(8,128)(2,1)}, u32[]{:S(2)}) copy-start(bf16[1,1024,3584]{2,1,0:T(8,128)(2,1)} %param.28) | copy-start | bytes 22020100
  21.5 28.0 %slice-start.2 = ((s8[7340032]{0:T(1024)(128)(4,1)}), s8[4194304]{0:T(1024)(128)(4,1)S(1)}, s32[]{:S(2)}) async-start(s8[7340032]{0:T(1024)(128)(4,1)} %bitcast.33), calls=%async_computation.2 | async-start | bytes 8388608
  21.5 28.0 %slice-start.4 = ((s8[7340032]{0:T(1024)(128)(4,1)}), s8[4194304]{0:T(1024)(128)(4,1)S(1)}, s32[]{:S(2)}) async-start(s8[7340032]{0:T(1024)(128)(4,1)} %bitcast.36), calls=%async_computation.4 | async-start | bytes 8388608
  31.1 18.4 %slice-start.3 = ((s8[7340032]{0:T(1024)(128)(4,1)}), s8[3145728]{0:T(1024)(128)(4,1)S(1)}, s32[]{:S(2)}) async-start(s8[7340032]{0:T(1024)(128)(4,1)} %bitcast.33), calls=%async_computation.3 | async-start | bytes 6291456
  31.1 18.4 %slice-start.5 = ((s8[7340032]{0:T(1024)(128)(4,1)}), s8[3145728]{0:T(1024)(128)(4,1)S(1)}, s32[]{:S(2)}) async-start(s8[7340032]{0:T(1024)(128)(4,1)} %bitcast.36), calls=%async_computation.5 | async-start | bytes 6291456
  31.1 18.4 %copy-start.1 = (bf16[1,1024,3584]{2,1,0:T(8,128)(2,1)S(1)}, bf16[1,1024,3584]{2,1,0:T(8,128)(2,1)}, u32[]{:S(2)}) copy-start(bf16[1,1024,3584]{2,1,0:T(8,128)(2,1)} %param.31) | copy-start | bytes 22020100
  40.9 3.7 %collective-permute-start.9 = (bf16[8,7168]{1,0:T(8,128)(2,1)S(1)}, bf16[8,7168]{1,0:T(8,128)(2,1)S(1)}, u32[]{:S(2)}, u32[]{:S(2)}) collective-permute-start(bf16[8,7168]{1,0:T(8,128)(2,1)S(1)} %get-tuple-element.66), channel_id=1, source_target_pairs={{0,1},{1,0},{2,3},{3,2},{4,5},{5,4},{6,7},{7,6},{8,9},{9,8},{10,11... | collective-permute-start | bytes 344072 | tf_op jit(solution)/shard_map/ppermute | solution.py:310
  41.1 5.7 %collective-permute-start.10 = (bf16[8,7168]{1,0:T(8,128)(2,1)S(1)}, bf16[8,7168]{1,0:T(8,128)(2,1)S(1)}, u32[]{:S(2)}, u32[]{:S(2)}) collective-permute-start(bf16[8,7168]{1,0:T(8,128)(2,1)S(1)} %get-tuple-element.67), channel_id=1, source_target_pairs={{0,2},{1,3},{2,0},{3,1},{4,6},{5,7},{6,4},{7,5},{8,10},{9,11},{10,... | collective-permute-start | bytes 344072 | tf_op jit(solution)/shard_map/ppermute | solution.py:310
  42.3 17.1 %collective-permute-start.11 = (bf16[8,7168]{1,0:T(8,128)(2,1)S(1)}, bf16[8,7168]{1,0:T(8,128)(2,1)S(1)}, u32[]{:S(2)}, u32[]{:S(2)}) collective-permute-start(bf16[8,7168]{1,0:T(8,128)(2,1)S(1)} %get-tuple-element.68), channel_id=1, source_target_pairs={{0,3},{1,2},{2,1},{3,0},{4,7},{5,6},{6,5},{7,4},{8,11},{9,10},{10,... | collective-permute-start | bytes 344072 | tf_op jit(solution)/shard_map/ppermute | solution.py:310
  43.1 16.3 %collective-permute-start.12 = (bf16[8,7168]{1,0:T(8,128)(2,1)S(1)}, bf16[8,7168]{1,0:T(8,128)(2,1)S(1)}, u32[]{:S(2)}, u32[]{:S(2)}) collective-permute-start(bf16[8,7168]{1,0:T(8,128)(2,1)S(1)} %get-tuple-element.69), channel_id=1, source_target_pairs={{0,4},{1,5},{2,6},{3,7},{4,0},{5,1},{6,2},{7,3},{8,12},{9,13},{10,... | collective-permute-start | bytes 344072 | tf_op jit(solution)/shard_map/ppermute | solution.py:310
  44.3 15.1 %collective-permute-start.13 = (bf16[8,7168]{1,0:T(8,128)(2,1)S(1)}, bf16[8,7168]{1,0:T(8,128)(2,1)S(1)}, u32[]{:S(2)}, u32[]{:S(2)}) collective-permute-start(bf16[8,7168]{1,0:T(8,128)(2,1)S(1)} %get-tuple-element.70), channel_id=1, source_target_pairs={{0,5},{1,4},{2,7},{3,6},{4,1},{5,0},{6,3},{7,2},{8,13},{9,12},{10,... | collective-permute-start | bytes 344072 | tf_op jit(solution)/shard_map/ppermute | solution.py:310
  44.6 14.8 %collective-permute-start.14 = (bf16[8,7168]{1,0:T(8,128)(2,1)S(1)}, bf16[8,7168]{1,0:T(8,128)(2,1)S(1)}, u32[]{:S(2)}, u32[]{:S(2)}) collective-permute-start(bf16[8,7168]{1,0:T(8,128)(2,1)S(1)} %get-tuple-element.71), channel_id=1, source_target_pairs={{0,6},{1,7},{2,4},{3,5},{4,2},{5,3},{6,0},{7,1},{8,14},{9,15},{10,... | collective-permute-start | bytes 344072 | tf_op jit(solution)/shard_map/ppermute | solution.py:310
  46.7 12.6 %collective-permute-start.15 = (bf16[8,7168]{1,0:T(8,128)(2,1)S(1)}, bf16[8,7168]{1,0:T(8,128)(2,1)S(1)}, u32[]{:S(2)}, u32[]{:S(2)}) collective-permute-start(bf16[8,7168]{1,0:T(8,128)(2,1)S(1)} %get-tuple-element.72), channel_id=1, source_target_pairs={{0,7},{1,6},{2,5},{3,4},{4,3},{5,2},{6,1},{7,0},{8,15},{9,14},{10,... | collective-permute-start | bytes 344072 | tf_op jit(solution)/shard_map/ppermute | solution.py:310

commit v3 on v2

--- a/solution.py
+++ b/solution.py
@@ -60,6 +60,8 @@
     capacity,
     groups,
     place_ref,
+    forward_hbm,
+    backward_hbm,
     fresh_hbm,
     turn_hbm,
     saved_hbm,
@@ -68,23 +70,22 @@
     aff_front_hbm,
     ids_back_hbm,
     aff_back_hbm,
+    even_ref,
+    odd_ref,
     fresh_ref,
     turn_ref,
     saved_ref,
     gain_ref,
-    rows_ref,
     front_table_ref,
     front_picks_ref,
     front_shares_ref,
     back_table_ref,
     back_picks_ref,
     slot_shares_ref,
-    ids_front_ref,
-    aff_front_ref,
-    ids_back_ref,
-    aff_back_ref,
-    sems,
+    *refs,
 ):
+    rows_refs = refs[:-7]
+    forward_ref, backward_ref, ids_front_ref, aff_front_ref, ids_back_ref, aff_back_ref, sems = refs[-7:]
     pairs = (
         (ids_front_hbm, ids_front_ref),
         (aff_front_hbm, aff_front_ref),
@@ -94,6 +95,8 @@
         (gain_hbm, gain_ref),
         (fresh_hbm, fresh_ref),
         (turn_hbm, turn_ref),
+        (forward_hbm, forward_ref),
+        (backward_hbm, backward_ref),
     )
     copies = [pltpu.make_async_copy(*pair, sems.at[i]) for i, pair in enumerate(pairs)]
     for copy in copies:
@@ -117,19 +120,23 @@
     copies[4].wait()
     copies[5].wait()
     _, normed = norm_rows(saved_ref[...].astype(F32), gain_ref[...].astype(F32))
-    rows_ref[...] = dot_nn(back_table_ref[...], normed).astype(BF16)
-    copies[6].wait()
-    copies[7].wait()
+    rows = dot_nn(back_table_ref[...], normed).astype(BF16)
+    for i, rows_ref in enumerate(rows_refs):
+        rows_ref[...] = rows[i * rows_ref.shape[0] : (i + 1) * rows_ref.shape[0]]
+    for copy in copies[6:]:
+        copy.wait()
+    even = place_ref[3] == 0
+    even_ref[...] = jnp.where(even, forward_ref[...].astype(F32), backward_ref[...].astype(F32)).astype(BF16)
+    odd_ref[...] = jnp.where(even, backward_ref[...].astype(F32), forward_ref[...].astype(F32)).astype(BF16)
 
 
 def pack_kernel(
     place_ref,
-    arrived_ref,
+    even_ref,
+    odd_ref,
     fresh_ref,
-    returned_ref,
     turn_ref,
     gain_ref,
-    rows_ref,
     front_table_ref,
     back_table_ref,
     slot_shares_ref,
@@ -138,19 +145,36 @@
     *packed_refs,
 ):
     width = fresh_ref.shape[1]
-    front = jnp.where(place_ref[0] == 0, fresh_ref[...].astype(F32), arrived_ref[...].astype(F32))
-    upstream = jnp.where(place_ref[1] == 0, turn_ref[...].astype(F32), returned_ref[...].astype(F32))
+    even = place_ref[3] == 0
+    by_even, by_odd = even_ref[...].astype(F32), odd_ref[...].astype(F32)
+    front = jnp.where(place_ref[0] == 0, fresh_ref[...].astype(F32), jnp.where(even, by_odd, by_even))
+    upstream = jnp.where(place_ref[1] == 0, turn_ref[...].astype(F32), jnp.where(even, by_even, by_odd))
     front_ref[...] = front.astype(BF16)
     upstream_ref[...] = upstream.astype(BF16)
     _, normed = norm_rows(front, gain_ref[...].astype(F32))
     front_rows = dot_nn(front_table_ref[...], normed).astype(BF16)
     grad_rows = (slot_shares_ref[...] * dot_nn(back_table_ref[...], upstream.astype(BF16))).astype(BF16)
-    back_rows = rows_ref[...]
     for i, packed_ref in enumerate(packed_refs):
         at = slice(i * packed_ref.shape[0], (i + 1) * packed_ref.shape[0])
         packed_ref[:, :width] = front_rows[at]
-        packed_ref[:, width : 2 * width] = back_rows[at]
-        packed_ref[:, 2 * width :] = grad_rows[at]
+        packed_ref[:, width:] = grad_rows[at]
+
+
+def split_kernel(pairs, after_hbm, *refs):
+    del after_hbm
+    keep_ref, give_ref = refs[pairs:]
+    values = [ref[...] for ref in refs[:pairs]]
+    half = values[0].shape[0] // 2
+    keep_ref[...] = jnp.concatenate([value[:half] for value in values], axis=0)
+    give_ref[...] = jnp.concatenate([value[half:] for value in values], axis=0)
+
+
+def merge_kernel(keep_ref, arrived_ref, *pair_refs):
+    keep, arrived = keep_ref[...], arrived_ref[...]
+    each = keep.shape[0] // len(pair_refs)
+    for i, pair_ref in enumerate(pair_refs):
+        at = slice(i * each, (i + 1) * each)
+        pair_ref[...] = jnp.concatenate([keep[at], arrived[at]], axis=0)
 
 
 def load_kernel(amount, *refs):
@@ -167,24 +191,27 @@
     chunk,
     tile,
     pieces,
+    halves,
     gate_ref,
     up_ref,
     down_ref,
     *refs,
 ):
-    rows_refs, refs = refs[:pieces], refs[pieces:]
+    rows_refs, back_refs, refs = refs[:pieces], refs[pieces : pieces + halves], refs[pieces + halves :]
     grads_ref, rows_t_ref, hidden_t_ref, dgate_ref, dup_ref = refs[:5]
-    parts_refs = refs[5 : 5 + pieces]
-    both_ref, grads_t_ref, dgate_t_ref, dup_t_ref, front_ref = refs[5 + pieces :]
+    parts_refs = refs[5 : 5 + halves]
+    both_ref, grads_t_ref, dgate_t_ref, dup_t_ref, front_ref = refs[5 + halves :]
     width, units = gate_ref.shape
     count = grads_ref.shape[0]
-    each = count // pieces
-    rows = jnp.concatenate([ref[...] for ref in rows_refs], axis=0)
+    each = count // halves
+    order = [i for half in range(halves) for i in range(half, pieces, halves)]
+    rows = jnp.concatenate([rows_refs[i][...] for i in order], axis=0)
     both_ref[:count] = rows[:, :width]
-    both_ref[count:] = rows[:, width : 2 * width]
-    grads_ref[...] = rows[:, 2 * width :]
-    rows_t_ref[...] = rows[:, width : 2 * width].T
-    grads_t_ref[...] = rows[:, 2 * width :].T
+    grads_ref[...] = rows[:, width:]
+    grads_t_ref[...] = rows[:, width:].T
+    rows = jnp.concatenate([ref[...] for ref in back_refs], axis=0)
+    both_ref[count:] = rows
+    rows_t_ref[...] = rows.T
     for i in range(units // chunk):
         at = slice(i * chunk, (i + 1) * chunk)
         gate_pre = dot_nn(both_ref[...], gate_ref[:, at])
@@ -213,27 +240,32 @@
             parts_ref[:, width + j * tile : width + (j + 1) * tile] = back[own]
 
 
-def grads_kernel(
-    wide,
-    deep,
-    rows_t_ref,
-    hidden_t_ref,
-    dgate_ref,
-    dup_ref,
-    grads_ref,
-    mgate_ref,
-    mup_ref,
-    mdown_ref,
-    ogate_ref,
-    oup_ref,
-    odown_ref,
-):
-    at = pl.ds(pl.multiple_of(pl.program_id(0) * wide, 16), wide)
-    rows_t = rows_t_ref[at, :]
-    ogate_ref[...] = (mgate_ref[at, :].astype(F32) + dot_nn(rows_t, dgate_ref[...])).astype(BF16)
-    oup_ref[...] = (mup_ref[at, :].astype(F32) + dot_nn(rows_t, dup_ref[...])).astype(BF16)
-    at = pl.ds(pl.multiple_of(pl.program_id(0) * deep, 16), deep)
-    odown_ref[...] = (mdown_ref[at, :].astype(F32) + dot_nn(hidden_t_ref[at, :], grads_ref[...])).astype(BF16)
+def grads_kernel(slots, tile, by_rows, after_hbm, *refs):
+    del after_hbm
+    amount = len(by_rows)
+    mirrors, lefts, rights, outs = (refs[i * amount : (i + 1) * amount] for i in range(4))
+    bufs, sems = refs[4 * amount : 5 * amount], refs[-1]
+    steps = [out.shape[0 if rows else 1] // tile for out, rows in zip(outs, by_rows)]
+
+    def copy(i, j):
+        at = pl.ds(i * tile, tile)
+        target = outs[j].at[at, :] if by_rows[j] else outs[j].at[:, at]
+        return pltpu.make_async_copy(bufs[j].at[i % slots], target, sems.at[j, i % slots])
+
+    for i in range(max(steps)):
+        for j in range(amount):
+            if i >= slots:
+                copy(i - slots, j).wait()
+            at = slice(i * tile, (i + 1) * tile)
+            if by_rows[j]:
+                total = mirrors[j][at, :].astype(F32) + dot_nn(lefts[j][at, :], rights[j][...])
+            else:
+                total = mirrors[j][:, at].astype(F32) + dot_nn(lefts[j][...], rights[j][:, at])
+            bufs[j][i % slots] = total.astype(BF16)
+            copy(i, j).start()
+    for j in range(amount):
+        for i in range(max(steps[j] - slots, 0), steps[j]):
+            copy(i, j).wait()
 
 
 def combine_kernel(
@@ -301,18 +333,77 @@
     )(after, *(in_hbm(a) for a in arrays))
 
 
-def exchanged(pieces):
+def exchanged(pieces, step=1):
     if len(pieces) == 1:
         peers = lax.axis_size("ep")
         rows = pieces[0].reshape(peers, -1, pieces[0].shape[-1])
         return (lax.all_to_all(rows, "ep", split_axis=0, concat_axis=0, tiled=True).reshape(pieces[0].shape),)
-    peers = range(len(pieces))
-    return (pieces[0],) + tuple(lax.ppermute(pieces[i], "ep", [(j, j ^ i) for j in peers]) for i in peers[1:])
-
-
-def ring(value, by):
+    peers = range(lax.axis_size("ep"))
+    order = range(len(pieces) - 1, 0, -1)
+    sent = {i: lax.ppermute(pieces[i], "ep", [(j, j ^ (i * step)) for j in peers]) for i in order}
+    return (pieces[0], *(sent[i] for i in range(1, len(pieces))))
+
+
+def swapped(halves):
+    if len(halves) == 1:
+        return halves
+    peers = range(lax.axis_size("ep"))
+    return halves[0], lax.ppermute(halves[1], "ep", [(j, j ^ 1) for j in peers])
+
+
+def split(pairs, after):
+    if len(pairs) == 1:
+        return pairs
+    count, width = pairs[0].shape
+    count = count * len(pairs) // 2
+    keep, give = pl.pallas_call(
+        functools.partial(split_kernel, len(pairs)),
+        out_shape=(shape((count, width)),) * 2,
+        in_specs=[whole(pl.ANY)] + [whole()] * len(pairs),
+        out_specs=(whole(),) * 2,
+        compiler_params=pltpu.CompilerParams(vmem_limit_bytes=4 * MIB),
+        cost_estimate=cost(0, 8 * count * width),
+        name="split_rows",
+    )(after, *pairs)
+    return swapped((keep, give))
+
+
+def merged(halves):
+    if len(halves) == 1:
+        return halves
+    count, width = halves[0].shape
+    return pl.pallas_call(
+        merge_kernel,
+        out_shape=(shape((count // 2, width)),) * 4,
+        in_specs=[whole()] * 2,
+        out_specs=(whole(),) * 4,
+        compiler_params=pltpu.CompilerParams(vmem_limit_bytes=4 * MIB),
+        cost_estimate=cost(0, 8 * count * width),
+        name="merge_rows",
+    )(*halves)
+
+
+def weight_grads(after, mirrors, lefts, rights, by_rows):
+    slots, tile = 4 // len(mirrors) + 1, 512
+    tiles = [(tile, m.shape[1]) if rows else (m.shape[0], tile) for m, rows in zip(mirrors, by_rows)]
+    size = sum(m.size for m in mirrors)
+    return pl.pallas_call(
+        functools.partial(grads_kernel, slots, tile, by_rows),
+        out_shape=tuple(shape(m.shape) for m in mirrors),
+        in_specs=[whole(pl.ANY)] + [whole()] * (3 * len(mirrors)),
+        out_specs=(whole(pl.ANY),) * len(mirrors),
+        scratch_shapes=[pltpu.VMEM((slots, *t), BF16) for t in tiles]
+        + [pltpu.SemaphoreType.DMA((len(mirrors), slots))],
+        compiler_params=pltpu.CompilerParams(vmem_limit_bytes=10 * MIB),
+        cost_estimate=cost(2 * size * rights[0].shape[0], 4 * size),
+        name="weight_grads",
+    )(after, *mirrors, *lefts, *rights)
+
+
+def beside(value, first):
     size = lax.axis_size("section")
-    return lax.ppermute(value, "section", [(i, (i + by) % size) for i in range(size)])
+    pairs = [(i, i + 1 if (i - first) % 2 == 0 else i - 1) for i in range(size)]
+    return lax.ppermute(value, "section", [(i, j if 0 <= j < size else i) for i, j in pairs])
 
 
 def body(
@@ -340,63 +431,65 @@
     count = peers * capacity
     units = w_gate.shape[2]
     section_id = lax.axis_index("section")
-    pieces = peers if peers <= 8 else 1
+    pieces, pairs, halves = (8, 4, 2) if peers == 8 else (1, 1, 1)
     flip = lax.axis_index("ep") if pieces > 1 else jnp.int32(0)
-    place = jnp.stack([section_id, lax.axis_size("section") - 1 - section_id, flip]).astype(jnp.int32)
-    returned = ring(sent_backward, -1)
-    arrived = ring(sent_forward, 1)
+    place = jnp.stack([section_id, lax.axis_size("section") - 1 - section_id, flip, section_id % 2]).astype(jnp.int32)
     early = pl.pallas_call(
         functools.partial(early_kernel, capacity, groups),
-        out_shape=(held((tokens, width)),) * 3
+        out_shape=(shape((tokens, width)),) * 2
+        + (held((tokens, width)),) * 3
         + (
             held((1, width)),
-            held((count, width)),
             held((count, tokens)),
             held((2, tokens, count)),
             held((2, tokens, 1), F32),
             held((count, tokens)),
             held((tokens, count)),
             held((count, 1), F32),
-        ),
-        in_specs=[whole(pltpu.SMEM)] + [whole(pl.ANY)] * 8,
-        out_specs=(whole(),) * 11,
-        scratch_shapes=[pltpu.VMEM((2, tokens), t) for t in (jnp.int32, F32, jnp.int32, F32)]
-        + [pltpu.SemaphoreType.DMA((8,))],
+        )
+        + (shape((count // pairs, width)),) * pairs,
+        in_specs=[whole(pltpu.SMEM)] + [whole(pl.ANY)] * 10,
+        out_specs=(whole(),) * (12 + pairs),
+        scratch_shapes=[pltpu.VMEM((tokens, width), BF16)] * 2
+        + [pltpu.VMEM((2, tokens), t) for t in (jnp.int32, F32, jnp.int32, F32)]
+        + [pltpu.SemaphoreType.DMA((10,))],
         compiler_params=pltpu.CompilerParams(vmem_limit_bytes=4 * MIB),
         cost_estimate=cost(2 * count * tokens * width, 2 * count * width),
         name="early_rows",
     )(
         place,
-        *(in_hbm(v) for v in (fresh_tokens, turn_gradient, saved_input[0], gain)),
+        *(in_hbm(v) for v in (sent_forward[0], sent_backward[0], fresh_tokens, turn_gradient, saved_input[0], gain)),
         *(in_hbm(v[0].T) for v in (ids_front, affinity_front, ids_back, affinity_back)),
     )
-    fresh, turn, saved, gain_row, back_rows = early[:5]
-    front_table, front_picks, front_shares, back_table, back_picks, slot_shares = early[5:]
+    by_even, by_odd = (beside(early[i], i) for i in range(2))
+    fresh, turn, saved, gain_row = early[2:6]
+    front_table, front_picks, front_shares, back_table, back_picks, slot_shares = early[6:12]
+    back_pairs = exchanged(early[12:], 2)
     front, upstream, *packed = pl.pallas_call(
         pack_kernel,
-        out_shape=(held((tokens, width)),) * 2 + (shape((count // pieces, 3 * width)),) * pieces,
-        in_specs=[whole(pltpu.SMEM)] + [whole()] * 9,
+        out_shape=(held((tokens, width)),) * 2 + (shape((count // pieces, 2 * width)),) * pieces,
+        in_specs=[whole(pltpu.SMEM)] + [whole()] * 8,
         out_specs=(whole(),) * (2 + pieces),
         compiler_params=pltpu.CompilerParams(vmem_limit_bytes=6 * MIB),
         cost_estimate=cost(2 * count * tokens * width * 4, 5 * count * width),
         name="pack_rows",
     )(
         place,
-        arrived[0],
+        by_even,
+        by_odd,
         fresh,
-        returned[0],
         turn,
         gain_row,
-        back_rows,
         front_table,
         back_table,
         slot_shares,
     )
     rows = exchanged(packed)
-    (w_gate,) = loaded(packed[0], w_gate[0])
+    (w_gate,) = loaded(rows[len(rows) * 3 // 8], w_gate[0])
+    back_rows = split(back_pairs, packed[0])
     chunk, tile = min(256, units), width // 7
     grads, rows_t, hidden_t, dgate, dup, *parts = pl.pallas_call(
-        functools.partial(expert_kernel, chunk, tile, pieces),
+        functools.partial(expert_kernel, chunk, tile, pieces, halves),
         out_shape=(
             held((count, width)),
             held((width, count)),
@@ -404,9 +497,9 @@
             held((count, units)),
             held((count, units)),
         )
-        + (shape((count // pieces, 2 * width)),) * pieces,
-        in_specs=[whole()] * (3 + pieces),
-        out_specs=(whole(),) * (5 + pieces),
+        + (shape((count // halves, 2 * width)),) * halves,
+        in_specs=[whole()] * (3 + pieces + halves),
+        out_specs=(whole(),) * (5 + halves),
         scratch_shapes=[
             pltpu.VMEM((2 * count, width), BF16),
             pltpu.VMEM((width, count), BF16),
@@ -417,26 +510,17 @@
         compiler_params=pltpu.CompilerParams(vmem_limit_bytes=(6 if count <= 128 else 32) * MIB),
         cost_estimate=cost(2 * count * width * units * 8, 6 * width * units),
         name="expert_rows",
-    )(w_gate, w_up[0], w_down[0], *rows)
-    back = exchanged(parts)
-    steps = 8
-    wide, deep = width // steps, units // steps
-    gate_spec = pl.BlockSpec((wide, units), lambda i: (i, 0))
-    down_spec = pl.BlockSpec((deep, width), lambda i: (i, 0))
-    out_gate, out_up, out_down = pl.pallas_call(
-        functools.partial(grads_kernel, wide, deep),
-        grid=(steps,),
-        out_shape=(shape((width, units)), shape((width, units)), shape((units, width))),
-        in_specs=[whole()] * 8,
-        out_specs=(gate_spec, gate_spec, down_spec),
-        compiler_params=pltpu.CompilerParams(vmem_limit_bytes=8 * MIB),
-        cost_estimate=cost(2 * count * width * units * 3, 12 * width * units),
-        name="weight_grads",
-    )(rows_t, hidden_t, dgate, dup, grads, mirror_gate[0], mirror_up[0], mirror_down[0])
+    )(w_gate, w_up[0], w_down[0], *rows, *back_rows)
+    neighbour = swapped(parts)
+    (out_gate,) = weight_grads(parts[0], (mirror_gate[0],), (rows_t,), (dgate,), (True,))
+    back = exchanged(merged(neighbour), 2)
+    out_up, out_down = weight_grads(
+        back[0], (mirror_up[0], mirror_down[0]), (rows_t, hidden_t), (dup, grads), (True, False)
+    )
     forward_out, grad_input = pl.pallas_call(
         combine_kernel,
         out_shape=(shape((tokens, width)), shape((tokens, width))),
-        in_specs=[whole()] * (7 + pieces),
+        in_specs=[whole()] * (7 + pairs),
         out_specs=(whole(),) * 2,
         compiler_params=pltpu.CompilerParams(vmem_limit_bytes=6 * MIB),
         cost_estimate=cost(2 * count * tokens * width * 3, 4 * count * width),

time: 60.7 us -> 55.7 us (0.918)
  the two profiles are of different devices: /device:TPU:1 before, /device:TPU:8 now
where the time goes in v3:
time: 55.7 us; the launch traced here: 55.5 us
  Pallas kernels  27 us (48%)
  starting transfers between devices  19.7 us (35%)
  waiting for transfers between devices  7.91 us (14%)
  between operations  0.88 us (2%)
    ppermute x13, starting transfers between devices, exchanged(): lax.ppermute(pieces[i], 'ep', [(j, j ^ i * step) for j in peers])  14.1 us
    pallas_call x1, Pallas kernels, body(): pl.pallas_call(functools.partial(expert_kernel, chunk, tile, pieces, halv...  9.68 us
    pallas_call x2, Pallas kernels, weight_grads(): pl.pallas_call(functools.partial(grads_kernel, slots, tile, by_rows), out...  9.58 us
    ppermute x13, waiting for transfers between devices, exchanged(): lax.ppermute(pieces[i], 'ep', [(j, j ^ i * step) for j in peers])  6.38 us
    ppermute x2, starting transfers between devices, beside(): lax.ppermute(value, 'section', [(i, j if 0 <= j < size else i) for i, j i...  5.11 us
    pallas_call x1, Pallas kernels, loaded(): pl.pallas_call(functools.partial(load_kernel, amount), out_shape=tuple((h...  3.24 us
    pallas_call x1, Pallas kernels, body(): pl.pallas_call(functools.partial(early_kernel, capacity, groups), out_sha...  2.07 us
    ppermute x2, waiting for transfers between devices, swapped(): lax.ppermute(halves[1], 'ep', [(j, j ^ 1) for j in peers])  1.53 us
  transfers between devices with their start and end apart: 17, of which 6 were waited for; matrix products, arithmetic and copies ran while one was open for 0% of the time, Pallas kernels for 25%

profile of v3, /device:TPU:8, one launch (start us, length us, event | category | flops | bytes accessed | tf_op | source)
XLA Modules:
  0.0 55.5 jit_solution(8866133124848251996)
XLA Ops:
  0.6 0.1 pad_add_fusion.place_ref
  0.7 2.1 %early_rows.1 = (bf16[16,3584]{1,0:T(8,128)(2,1)S(1)}, bf16[16,3584]{1,0:T(8,128)(2,1)S(1)}, bf16[16,3584]{1,0:T(8,128)(2,1)S(1)}, bf16[16,3584]{1,0:T(8,128)(2,...) custom-call(s32[4]{0:T(128)S(1)} %pad_add_fusion.place_ref, ...), custom_call_target="tpu_custom_call" | custom-call | flops 7340032 | bytes 458752 | tf_op jit(solution)/shard_map/early_rows/pallas_call | solution.py:437
  2.8 0.1 collective-permute-start
  2.9 5.0 %collective-permute-start.1 = (bf16[16,3584]{1,0:T(8,128)(2,1)S(1)}, bf16[16,3584]{1,0:T(8,128)(2,1)S(1)}, u32[]{:S(2)}, u32[]{:S(2)}) collective-permute-start(bf16[16,3584]{1,0:T(8,128)(2,1)S(1)} %get-tuple-element.49), channel_id=1, source_target_pairs={{0,0},{8,16},{16,8},{24,24},{1,1},{9,17},{17,9},{25,25},{2,2},{10,... | collective-permute-start | bytes 344072 | tf_op jit(solution)/shard_map/ppermute | solution.py:406
  7.9 1.6 %collective-permute-start.9 = (bf16[16,3584]{1,0:T(8,128)(2,1)S(1)}, bf16[16,3584]{1,0:T(8,128)(2,1)S(1)}, u32[]{:S(2)}, u32[]{:S(2)}) collective-permute-start(bf16[16,3584]{1,0:T(8,128)(2,1)S(1)} %get-tuple-element.71), channel_id=1, source_target_pairs={{0,2},{1,3},{2,0},{3,1},{4,6},{5,7},{6,4},{7,5},{8,10},{9,11},{10,... | collective-permute-start | bytes 344072 | tf_op jit(solution)/shard_map/ppermute | solution.py:343
  9.5 1.5 %collective-permute-start.10 = (bf16[16,3584]{1,0:T(8,128)(2,1)S(1)}, bf16[16,3584]{1,0:T(8,128)(2,1)S(1)}, u32[]{:S(2)}, u32[]{:S(2)}) collective-permute-start(bf16[16,3584]{1,0:T(8,128)(2,1)S(1)} %get-tuple-element.72), channel_id=1, source_target_pairs={{0,4},{1,5},{2,6},{3,7},{4,0},{5,1},{6,2},{7,3},{8,12},{9,13},{10,... | collective-permute-start | bytes 344072 | tf_op jit(solution)/shard_map/ppermute | solution.py:343
  11.0 0.5 collective-permute-start.11
  11.5 0.0 collective-permute-done.even_ref
  11.5 0.0 collective-permute-done.1.odd_ref
  11.5 1.1 %pack_rows.1 = (bf16[16,3584]{1,0:T(8,128)(2,1)S(1)}, bf16[16,3584]{1,0:T(8,128)(2,1)S(1)}, bf16[8,7168]{1,0:T(8,128)(2,1)S(1)}, bf16[8,7168]{1,0:T(8,128)(2,1)S...) custom-call(s32[4]{0:T(128)S(1)} %pad_add_fusion.place_ref, ...), custom_call_target="tpu_custom_call" | custom-call | flops 29360128 | bytes 1146880 | tf_op jit(solution)/shard_map/pack_rows/pallas_call | solution.py:468
  12.6 0.1 collective-permute-start.2
  12.7 1.6 %collective-permute-start.3 = (bf16[8,7168]{1,0:T(8,128)(2,1)S(1)}, bf16[8,7168]{1,0:T(8,128)(2,1)S(1)}, u32[]{:S(2)}, u32[]{:S(2)}) collective-permute-start(bf16[8,7168]{1,0:T(8,128)(2,1)S(1)} %get-tuple-element.64), channel_id=1, source_target_pairs={{0,1},{1,0},{2,3},{3,2},{4,5},{5,4},{6,7},{7,6},{8,9},{9,8},{10,11... | collective-permute-start | bytes 344072 | tf_op jit(solution)/shard_map/ppermute | solution.py:343
  14.3 0.0 collective-permute-done.9.refs_1_
  14.3 1.0 %collective-permute-start.4 = (bf16[8,7168]{1,0:T(8,128)(2,1)S(1)}, bf16[8,7168]{1,0:T(8,128)(2,1)S(1)}, u32[]{:S(2)}, u32[]{:S(2)}) collective-permute-start(bf16[8,7168]{1,0:T(8,128)(2,1)S(1)} %get-tuple-element.65), channel_id=1, source_target_pairs={{0,2},{1,3},{2,0},{3,1},{4,6},{5,7},{6,4},{7,5},{8,10},{9,11},{10,... | collective-permute-start | bytes 344072 | tf_op jit(solution)/shard_map/ppermute | solution.py:343
  15.2 0.6 %collective-permute-done.10.refs_2_ = bf16[16,3584]{1,0:T(8,128)(2,1)S(1)} collective-permute-done((bf16[16,3584]{1,0:T(8,128)(2,1)S(1)}, bf16[16,3584]{1,0:T(8,128)(2,1)S(1)}, u32[]{:S(2)}, u32[]{:S(2)}) %collective-permute-start.10) | collective-permute-done | bytes 114720 | tf_op jit(solution)/shard_map/ppermute | solution.py:343
  15.8 0.9 %collective-permute-done.11.refs_3_ = bf16[16,3584]{1,0:T(8,128)(2,1)S(1)} collective-permute-done((bf16[16,3584]{1,0:T(8,128)(2,1)S(1)}, bf16[16,3584]{1,0:T(8,128)(2,1)S(1)}, u32[]{:S(2)}, u32[]{:S(2)}) %collective-permute-start.11) | collective-permute-done | bytes 114720 | tf_op jit(solution)/shard_map/ppermute | solution.py:343
  16.8 0.1 split_rows.1
  16.8 0.1 collective-permute-start.12
  16.9 1.1 %collective-permute-start.5 = (bf16[8,7168]{1,0:T(8,128)(2,1)S(1)}, bf16[8,7168]{1,0:T(8,128)(2,1)S(1)}, u32[]{:S(2)}, u32[]{:S(2)}) collective-permute-start(bf16[8,7168]{1,0:T(8,128)(2,1)S(1)} %get-tuple-element.66), channel_id=1, source_target_pairs={{0,4},{1,5},{2,6},{3,7},{4,0},{5,1},{6,2},{7,3},{8,12},{9,13},{10,... | collective-permute-start | bytes 344072 | tf_op jit(solution)/shard_map/ppermute | solution.py:343
  18.0 0.1 collective-permute-done.2.refs_0_.refs_3_
  18.1 1.2 %collective-permute-start.6 = (bf16[8,7168]{1,0:T(8,128)(2,1)S(1)}, bf16[8,7168]{1,0:T(8,128)(2,1)S(1)}, u32[]{:S(2)}, u32[]{:S(2)}) collective-permute-start(bf16[8,7168]{1,0:T(8,128)(2,1)S(1)} %get-tuple-element.67), channel_id=1, source_target_pairs={{0,5},{1,4},{2,7},{3,6},{4,1},{5,0},{6,3},{7,2},{8,13},{9,12},{10,... | collective-permute-start | bytes 344072 | tf_op jit(solution)/shard_map/ppermute | solution.py:343
  19.3 0.0 collective-permute-done.3.refs_1_
  19.4 0.6 %collective-permute-start.7 = (bf16[8,7168]{1,0:T(8,128)(2,1)S(1)}, bf16[8,7168]{1,0:T(8,128)(2,1)S(1)}, u32[]{:S(2)}, u32[]{:S(2)}) collective-permute-start(bf16[8,7168]{1,0:T(8,128)(2,1)S(1)} %get-tuple-element.68), channel_id=1, source_target_pairs={{0,6},{1,7},{2,4},{3,5},{4,2},{5,3},{6,0},{7,1},{8,14},{9,15},{10,... | collective-permute-start | bytes 344072 | tf_op jit(solution)/shard_map/ppermute | solution.py:343
  19.9 0.7 %collective-permute-done.4.refs_2_ = bf16[8,7168]{1,0:T(8,128)(2,1)S(1)} collective-permute-done((bf16[8,7168]{1,0:T(8,128)(2,1)S(1)}, bf16[8,7168]{1,0:T(8,128)(2,1)S(1)}, u32[]{:S(2)}, u32[]{:S(2)}) %collective-permute-start.4) | collective-permute-done | bytes 114720 | tf_op jit(solution)/shard_map/ppermute | solution.py:343
  20.6 1.4 %collective-permute-start.8 = (bf16[8,7168]{1,0:T(8,128)(2,1)S(1)}, bf16[8,7168]{1,0:T(8,128)(2,1)S(1)}, u32[]{:S(2)}, u32[]{:S(2)}) collective-permute-start(bf16[8,7168]{1,0:T(8,128)(2,1)S(1)} %get-tuple-element.69), channel_id=1, source_target_pairs={{0,7},{1,6},{2,5},{3,4},{4,3},{5,2},{6,1},{7,0},{8,15},{9,14},{10,... | collective-permute-start | bytes 344072 | tf_op jit(solution)/shard_map/ppermute | solution.py:343
  22.1 3.2 %load_weights.1.gate_ref = bf16[3584,1024]{1,0:T(8,128)(2,1)S(1)} custom-call(bf16[8,7168]{1,0:T(8,128)(2,1)S(1)} %collective-permute-done.2.refs_0_.refs_3_, bf16[3584,1024]{1,0:T(8,128)(2,1)} %bitcast.43), custom_call_target="tpu_custom_call" | custom-call | bytes 7340032 | tf_op jit(solution)/shard_map/load_weights/pallas_call | solution.py:324
  25.3 0.0 collective-permute-done.5.refs_4_
  25.3 4.1 %collective-permute-done.6.refs_5_ = bf16[8,7168]{1,0:T(8,128)(2,1)S(1)} collective-permute-done((bf16[8,7168]{1,0:T(8,128)(2,1)S(1)}, bf16[8,7168]{1,0:T(8,128)(2,1)S(1)}, u32[]{:S(2)}, u32[]{:S(2)}) %collective-permute-start.6) | collective-permute-done | bytes 114720 | tf_op jit(solution)/shard_map/ppermute | solution.py:343
  29.4 0.0 collective-permute-done.7.refs_6_
  29.4 0.0 collective-permute-done.8.refs_7_
  29.4 0.0 collective-permute-done.12.refs_9_
  29.4 0.0 slice-start.3
  29.5 0.0 slice-start.7
  29.5 9.7 %expert_rows.1 = (bf16[64,3584]{1,0:T(8,128)(2,1)S(1)}, bf16[3584,64]{1,0:T(8,128)(2,1)S(1)}, bf16[1024,64]{1,0:T(8,128)(2,1)S(1)}, bf16[64,1024]{1,0:T(8,128)(2...) custom-call(bf16[3584,1024]{1,0:T(8,128)(2,1)S(1)} %load_weights.1.gate_ref, ...), custom_call_target="tpu_custom_call" | custom-call | flops 3758096384 | bytes 22020096 | tf_op jit(solution)/shard_map/expert_rows/pallas_call | solution.py:491
  39.2 0.4 collective-permute-start.13
  39.5 1.5 %collective-permute-done.13.arrived_ref = bf16[32,7168]{1,0:T(8,128)(2,1)S(1)} collective-permute-done((bf16[32,7168]{1,0:T(8,128)(2,1)S(1)}, bf16[32,7168]{1,0:T(8,128)(2,1)S(1)}, u32[]{:S(2)}, u32[]{:S(2)}) %collective-permute-start.13) | collective-permute-done | bytes 458784 | tf_op jit(solution)/shard_map/ppermute | solution.py:351
  41.0 0.1 merge_rows.1
  41.2 0.8 %collective-permute-start.14 = (bf16[16,7168]{1,0:T(8,128)(2,1)S(1)}, bf16[16,7168]{1,0:T(8,128)(2,1)S(1)}, u32[]{:S(2)}, u32[]{:S(2)}) collective-permute-start(bf16[16,7168]{1,0:T(8,128)(2,1)S(1)} %get-tuple-element.79), channel_id=1, source_target_pairs={{0,2},{1,3},{2,0},{3,1},{4,6},{5,7},{6,4},{7,5},{8,10},{9,11},{10,... | collective-permute-start | bytes 688136 | tf_op jit(solution)/shard_map/ppermute | solution.py:343
  42.0 0.8 %collective-permute-start.15 = (bf16[16,7168]{1,0:T(8,128)(2,1)S(1)}, bf16[16,7168]{1,0:T(8,128)(2,1)S(1)}, u32[]{:S(2)}, u32[]{:S(2)}) collective-permute-start(bf16[16,7168]{1,0:T(8,128)(2,1)S(1)} %get-tuple-element.80), channel_id=1, source_target_pairs={{0,4},{1,5},{2,6},{3,7},{4,0},{5,1},{6,2},{7,3},{8,12},{9,13},{10,... | collective-permute-start | bytes 688136 | tf_op jit(solution)/shard_map/ppermute | solution.py:343
  42.8 2.0 %collective-permute-start.16 = (bf16[16,7168]{1,0:T(8,128)(2,1)S(1)}, bf16[16,7168]{1,0:T(8,128)(2,1)S(1)}, u32[]{:S(2)}, u32[]{:S(2)}) collective-permute-start(bf16[16,7168]{1,0:T(8,128)(2,1)S(1)} %get-tuple-element.81), channel_id=1, source_target_pairs={{0,6},{1,7},{2,4},{3,5},{4,2},{5,3},{6,0},{7,1},{8,14},{9,15},{10,... | collective-permute-start | bytes 688136 | tf_op jit(solution)/shard_map/ppermute | solution.py:343
  44.7 3.5 %weight_grads.2 = bf16[3584,1024]{1,0:T(8,128)(2,1)} custom-call(bf16[32,7168]{1,0:T(8,128)(2,1)S(1)} %get-tuple-element.76.keep_ref.after_hbm, bf16[3584,1024]{1,0:T(8,128)(2,1)S(1)} %bitcast.36, bf16[3584,64]{1,0:T(8,128)(2,1)S(1)} %get-tuple-element.84.refs_1_.refs_2_, bf16[64,1024]{1,0:T(8,128)(2,1)S(1)} %get-tuple-element.85.refs_2_), custom_call_target="tpu_custom_call" | custom-call | flops 469762048 | bytes 14680064 | tf_op jit(solution)/shard_map/weight_grads/pallas_call | solution.py:390
  48.3 0.0 slice-done.6
  48.3 0.0 slice-done.7
  48.3 6.1 %weight_grads.3 = (bf16[3584,1024]{1,0:T(8,128)(2,1)}, bf16[1024,3584]{1,0:T(8,128)(2,1)}) custom-call(bf16[16,7168]{1,0:T(8,128)(2,1)S(1)} %get-tuple-element.78.refs_0_.after_hbm, bf16[3584,1024]{1,0:T(8,128)(2,1)S(1)} %bitcast.39, bf16[1024,3584]{1,0:T(8,128)(2,1)S(1)} %bitcast.42, bf16[3584,64]{1,0:T(8,128)(2,1)S(1)} %get-tuple-element.84.refs_1_.refs_2_, ...), custom_call_target="tpu_custom_call" | custom-call | flops 939524096 | bytes 29360128 | tf_op jit(solution)/shard_map/weight_grads/pallas_call | solution.py:390
  54.4 0.0 collective-permute-done.14.refs_1_
  54.4 0.0 collective-permute-done.15.refs_2_
  54.4 0.0 collective-permute-done.16.refs_3_
  54.4 1.1 %combine_rows.1 = (bf16[16,3584]{1,0:T(8,128)(2,1)}, bf16[16,3584]{1,0:T(8,128)(2,1)}) custom-call(bf16[16,3584]{1,0:T(8,128)(2,1)S(1)} %get-tuple-element.56.front_ref, bf16[16,3584]{1,0:T(8,128)(2,1)S(1)} %get-tuple-element.57.upstream_ref, bf16[16,3584]{1,0:T(8,128)(2,1)S(1)} %get-tuple-element.58.saved_ref, ...), custom_call_target="tpu_custom_call" | custom-call | flops 22020096 | bytes 917504 | tf_op jit(solution)/shard_map/combine_rows/pallas_call | solution.py:520
  (18 shorter events, 0.0 us)
Async XLA Ops:
  2.8 8.7 %collective-permute-start = (bf16[16,3584]{1,0:T(8,128)(2,1)S(1)}, bf16[16,3584]{1,0:T(8,128)(2,1)S(1)}, u32[]{:S(2)}, u32[]{:S(2)}) collective-permute-start(bf16[16,3584]{1,0:T(8,128)(2,1)S(1)} %get-tuple-element.48), channel_id=1, source_target_pairs={{0,8},{8,0},{16,24},{24,16},{1,9},{9,1},{17,25},{25,17},{2,10},{10... | collective-permute-start | bytes 344072 | tf_op jit(solution)/shard_map/ppermute | solution.py:406
  2.9 8.6 %collective-permute-start.1 = (bf16[16,3584]{1,0:T(8,128)(2,1)S(1)}, bf16[16,3584]{1,0:T(8,128)(2,1)S(1)}, u32[]{:S(2)}, u32[]{:S(2)}) collective-permute-start(bf16[16,3584]{1,0:T(8,128)(2,1)S(1)} %get-tuple-element.49), channel_id=1, source_target_pairs={{0,0},{8,16},{16,8},{24,24},{1,1},{9,17},{17,9},{25,25},{2,2},{10,... | collective-permute-start | bytes 344072 | tf_op jit(solution)/shard_map/ppermute | solution.py:406
  7.9 6.3 %collective-permute-start.9 = (bf16[16,3584]{1,0:T(8,128)(2,1)S(1)}, bf16[16,3584]{1,0:T(8,128)(2,1)S(1)}, u32[]{:S(2)}, u32[]{:S(2)}) collective-permute-start(bf16[16,3584]{1,0:T(8,128)(2,1)S(1)} %get-tuple-element.71), channel_id=1, source_target_pairs={{0,2},{1,3},{2,0},{3,1},{4,6},{5,7},{6,4},{7,5},{8,10},{9,11},{10,... | collective-permute-start | bytes 344072 | tf_op jit(solution)/shard_map/ppermute | solution.py:343
  9.5 6.4 %collective-permute-start.10 = (bf16[16,3584]{1,0:T(8,128)(2,1)S(1)}, bf16[16,3584]{1,0:T(8,128)(2,1)S(1)}, u32[]{:S(2)}, u32[]{:S(2)}) collective-permute-start(bf16[16,3584]{1,0:T(8,128)(2,1)S(1)} %get-tuple-element.72), channel_id=1, source_target_pairs={{0,4},{1,5},{2,6},{3,7},{4,0},{5,1},{6,2},{7,3},{8,12},{9,13},{10,... | collective-permute-start | bytes 344072 | tf_op jit(solution)/shard_map/ppermute | solution.py:343
  11.0 5.8 %collective-permute-start.11 = (bf16[16,3584]{1,0:T(8,128)(2,1)S(1)}, bf16[16,3584]{1,0:T(8,128)(2,1)S(1)}, u32[]{:S(2)}, u32[]{:S(2)}) collective-permute-start(bf16[16,3584]{1,0:T(8,128)(2,1)S(1)} %get-tuple-element.73), channel_id=1, source_target_pairs={{0,6},{1,7},{2,4},{3,5},{4,2},{5,3},{6,0},{7,1},{8,14},{9,15},{10,... | collective-permute-start | bytes 344072 | tf_op jit(solution)/shard_map/ppermute | solution.py:343
  12.6 5.5 %collective-permute-start.2 = (bf16[8,7168]{1,0:T(8,128)(2,1)S(1)}, bf16[8,7168]{1,0:T(8,128)(2,1)S(1)}, u32[]{:S(2)}, u32[]{:S(2)}) collective-permute-start(bf16[8,7168]{1,0:T(8,128)(2,1)S(1)} %get-tuple-element.62), channel_id=1, source_target_pairs={{0,3},{1,2},{2,1},{3,0},{4,7},{5,6},{6,5},{7,4},{8,11},{9,10},{10,... | collective-permute-start | bytes 344072 | tf_op jit(solution)/shard_map/ppermute | solution.py:343
  12.7 6.7 %collective-permute-start.3 = (bf16[8,7168]{1,0:T(8,128)(2,1)S(1)}, bf16[8,7168]{1,0:T(8,128)(2,1)S(1)}, u32[]{:S(2)}, u32[]{:S(2)}) collective-permute-start(bf16[8,7168]{1,0:T(8,128)(2,1)S(1)} %get-tuple-element.64), channel_id=1, source_target_pairs={{0,1},{1,0},{2,3},{3,2},{4,5},{5,4},{6,7},{7,6},{8,9},{9,8},{10,11... | collective-permute-start | bytes 344072 | tf_op jit(solution)/shard_map/ppermute | solution.py:343
  14.3 6.4 %collective-permute-start.4 = (bf16[8,7168]{1,0:T(8,128)(2,1)S(1)}, bf16[8,7168]{1,0:T(8,128)(2,1)S(1)}, u32[]{:S(2)}, u32[]{:S(2)}) collective-permute-start(bf16[8,7168]{1,0:T(8,128)(2,1)S(1)} %get-tuple-element.65), channel_id=1, source_target_pairs={{0,2},{1,3},{2,0},{3,1},{4,6},{5,7},{6,4},{7,5},{8,10},{9,11},{10,... | collective-permute-start | bytes 344072 | tf_op jit(solution)/shard_map/ppermute | solution.py:343
  16.8 12.6 %slice-start = ((s8[7340032]{0:T(1024)(128)(4,1)}), s8[4194304]{0:T(1024)(128)(4,1)S(1)}, s32[]{:S(2)}) async-start(s8[7340032]{0:T(1024)(128)(4,1)} %bitcast.30), calls=%async_computation | async-start | bytes 8388608
  16.8 12.6 %collective-permute-start.12 = (bf16[32,3584]{1,0:T(8,128)(2,1)S(1)}, bf16[32,3584]{1,0:T(8,128)(2,1)S(1)}, u32[]{:S(2)}, u32[]{:S(2)}) collective-permute-start(bf16[32,3584]{1,0:T(8,128)(2,1)S(1)} %get-tuple-element.75), channel_id=1, source_target_pairs={{0,1},{1,0},{2,3},{3,2},{4,5},{5,4},{6,7},{7,6},{8,9},{9,8},{10,11... | collective-permute-start | bytes 688136 | tf_op jit(solution)/shard_map/ppermute | solution.py:351
  16.9 8.4 %collective-permute-start.5 = (bf16[8,7168]{1,0:T(8,128)(2,1)S(1)}, bf16[8,7168]{1,0:T(8,128)(2,1)S(1)}, u32[]{:S(2)}, u32[]{:S(2)}) collective-permute-start(bf16[8,7168]{1,0:T(8,128)(2,1)S(1)} %get-tuple-element.66), channel_id=1, source_target_pairs={{0,4},{1,5},{2,6},{3,7},{4,0},{5,1},{6,2},{7,3},{8,12},{9,13},{10,... | collective-permute-start | bytes 344072 | tf_op jit(solution)/shard_map/ppermute | solution.py:343
  18.1 11.3 %collective-permute-start.6 = (bf16[8,7168]{1,0:T(8,128)(2,1)S(1)}, bf16[8,7168]{1,0:T(8,128)(2,1)S(1)}, u32[]{:S(2)}, u32[]{:S(2)}) collective-permute-start(bf16[8,7168]{1,0:T(8,128)(2,1)S(1)} %get-tuple-element.67), channel_id=1, source_target_pairs={{0,5},{1,4},{2,7},{3,6},{4,1},{5,0},{6,3},{7,2},{8,13},{9,12},{10,... | collective-permute-start | bytes 344072 | tf_op jit(solution)/shard_map/ppermute | solution.py:343
  19.4 10.0 %collective-permute-start.7 = (bf16[8,7168]{1,0:T(8,128)(2,1)S(1)}, bf16[8,7168]{1,0:T(8,128)(2,1)S(1)}, u32[]{:S(2)}, u32[]{:S(2)}) collective-permute-start(bf16[8,7168]{1,0:T(8,128)(2,1)S(1)} %get-tuple-element.68), channel_id=1, source_target_pairs={{0,6},{1,7},{2,4},{3,5},{4,2},{5,3},{6,0},{7,1},{8,14},{9,15},{10,... | collective-permute-start | bytes 344072 | tf_op jit(solution)/shard_map/ppermute | solution.py:343
  20.6 8.8 %collective-permute-start.8 = (bf16[8,7168]{1,0:T(8,128)(2,1)S(1)}, bf16[8,7168]{1,0:T(8,128)(2,1)S(1)}, u32[]{:S(2)}, u32[]{:S(2)}) collective-permute-start(bf16[8,7168]{1,0:T(8,128)(2,1)S(1)} %get-tuple-element.69), channel_id=1, source_target_pairs={{0,7},{1,6},{2,5},{3,4},{4,3},{5,2},{6,1},{7,0},{8,15},{9,14},{10,... | collective-permute-start | bytes 344072 | tf_op jit(solution)/shard_map/ppermute | solution.py:343
  22.1 7.4 %slice-start.1 = ((s8[7340032]{0:T(1024)(128)(4,1)}), s8[3145728]{0:T(1024)(128)(4,1)S(1)}, s32[]{:S(2)}) async-start(s8[7340032]{0:T(1024)(128)(4,1)} %bitcast.30), calls=%async_computation.1 | async-start | bytes 6291456
  22.1 7.4 %copy-start = (bf16[1,1024,3584]{2,1,0:T(8,128)(2,1)S(1)}, bf16[1,1024,3584]{2,1,0:T(8,128)(2,1)}, u32[]{:S(2)}) copy-start(bf16[1,1024,3584]{2,1,0:T(8,128)(2,1)} %param.28) | copy-start | bytes 22020100
  22.1 22.7 %slice-start.2 = ((s8[7340032]{0:T(1024)(128)(4,1)}), s8[4194304]{0:T(1024)(128)(4,1)S(1)}, s32[]{:S(2)}) async-start(s8[7340032]{0:T(1024)(128)(4,1)} %bitcast.34), calls=%async_computation.2 | async-start | bytes 8388608
  22.1 26.2 %slice-start.6 = ((s8[7340032]{0:T(1024)(128)(4,1)}), s8[4194304]{0:T(1024)(128)(4,1)S(1)}, s32[]{:S(2)}) async-start(s8[7340032]{0:T(1024)(128)(4,1)} %bitcast.40), calls=%async_computation.6 | async-start | bytes 8388608
  29.4 15.3 %slice-start.3 = ((s8[7340032]{0:T(1024)(128)(4,1)}), s8[3145728]{0:T(1024)(128)(4,1)S(1)}, s32[]{:S(2)}) async-start(s8[7340032]{0:T(1024)(128)(4,1)} %bitcast.34), calls=%async_computation.3 | async-start | bytes 6291456
  29.5 18.8 %slice-start.7 = ((s8[7340032]{0:T(1024)(128)(4,1)}), s8[3145728]{0:T(1024)(128)(4,1)S(1)}, s32[]{:S(2)}) async-start(s8[7340032]{0:T(1024)(128)(4,1)} %bitcast.40), calls=%async_computation.7 | async-start | bytes 6291456
  39.2 1.9 %collective-permute-start.13 = (bf16[32,7168]{1,0:T(8,128)(2,1)S(1)}, bf16[32,7168]{1,0:T(8,128)(2,1)S(1)}, u32[]{:S(2)}, u32[]{:S(2)}) collective-permute-start(bf16[32,7168]{1,0:T(8,128)(2,1)S(1)} %get-tuple-element.77), channel_id=1, source_target_pairs={{0,1},{1,0},{2,3},{3,2},{4,5},{5,4},{6,7},{7,6},{8,9},{9,8},{10,11... | collective-permute-start | bytes 1376264 | tf_op jit(solution)/shard_map/ppermute | solution.py:351
  41.0 7.2 %slice-start.4 = ((s8[7340032]{0:T(1024)(128)(4,1)}), s8[4194304]{0:T(1024)(128)(4,1)S(1)}, s32[]{:S(2)}) async-start(s8[7340032]{0:T(1024)(128)(4,1)} %bitcast.37), calls=%async_computation.4 | async-start | bytes 8388608
  41.2 13.2 %collective-permute-start.14 = (bf16[16,7168]{1,0:T(8,128)(2,1)S(1)}, bf16[16,7168]{1,0:T(8,128)(2,1)S(1)}, u32[]{:S(2)}, u32[]{:S(2)}) collective-permute-start(bf16[16,7168]{1,0:T(8,128)(2,1)S(1)} %get-tuple-element.79), channel_id=1, source_target_pairs={{0,2},{1,3},{2,0},{3,1},{4,6},{5,7},{6,4},{7,5},{8,10},{9,11},{10,... | collective-permute-start | bytes 688136 | tf_op jit(solution)/shard_map/ppermute | solution.py:343
  42.0 12.5 %collective-permute-start.15 = (bf16[16,7168]{1,0:T(8,128)(2,1)S(1)}, bf16[16,7168]{1,0:T(8,128)(2,1)S(1)}, u32[]{:S(2)}, u32[]{:S(2)}) collective-permute-start(bf16[16,7168]{1,0:T(8,128)(2,1)S(1)} %get-tuple-element.80), channel_id=1, source_target_pairs={{0,4},{1,5},{2,6},{3,7},{4,0},{5,1},{6,2},{7,3},{8,12},{9,13},{10,... | collective-permute-start | bytes 688136 | tf_op jit(solution)/shard_map/ppermute | solution.py:343
  42.8 11.7 %collective-permute-start.16 = (bf16[16,7168]{1,0:T(8,128)(2,1)S(1)}, bf16[16,7168]{1,0:T(8,128)(2,1)S(1)}, u32[]{:S(2)}, u32[]{:S(2)}) collective-permute-start(bf16[16,7168]{1,0:T(8,128)(2,1)S(1)} %get-tuple-element.81), channel_id=1, source_target_pairs={{0,6},{1,7},{2,4},{3,5},{4,2},{5,3},{6,0},{7,1},{8,14},{9,15},{10,... | collective-permute-start | bytes 688136 | tf_op jit(solution)/shard_map/ppermute | solution.py:343
  44.7 3.6 %slice-start.5 = ((s8[7340032]{0:T(1024)(128)(4,1)}), s8[3145728]{0:T(1024)(128)(4,1)S(1)}, s32[]{:S(2)}) async-start(s8[7340032]{0:T(1024)(128)(4,1)} %bitcast.37), calls=%async_computation.5 | async-start | bytes 6291456

commit v4 on v3

--- a/solution.py
+++ b/solution.py
@@ -280,7 +280,7 @@
 ):
     forward_ref, input_ref = refs[-2:]
     width = front_ref.shape[1]
-    both = jnp.concatenate([ref[...] for ref in refs[:-2]], axis=0)
+    both = jnp.concatenate([refs[i][...] for i in ((0, 2, 3, 1) if len(refs) == 6 else (0,))], axis=0)
     parts = both[:, :width]
     forward_ref[...] = (
         front_ref[...].astype(F32)
@@ -525,7 +525,7 @@
         compiler_params=pltpu.CompilerParams(vmem_limit_bytes=6 * MIB),
         cost_estimate=cost(2 * count * tokens * width * 3, 4 * count * width),
         name="combine_rows",
-    )(front, upstream, saved, gain_row, front_picks, front_shares, back_picks, *back)
+    )(front, upstream, saved, gain_row, front_picks, front_shares, back_picks, *(back[i] for i in ((0, 3, 1, 2) if pairs == 4 else (0,))))
     return (forward_out[None], grad_input[None], out_gate[None], out_up[None], out_down[None])
 
 

time: 55.7 us -> 56.3 us (1.011)
  the two profiles are of different devices: /device:TPU:8 before, /device:TPU:9 now
where the time goes in v4:
time: 56.3 us; the launch traced here: 56.1 us
  Pallas kernels  27 us (48%)
  starting transfers between devices  20.8 us (37%)
  waiting for transfers between devices  7.37 us (13%)
  between operations  0.85 us (2%)
    ppermute x13, starting transfers between devices, exchanged(): lax.ppermute(pieces[i], 'ep', [(j, j ^ i * step) for j in peers])  13.5 us
    pallas_call x1, Pallas kernels, body(): pl.pallas_call(functools.partial(expert_kernel, chunk, tile, pieces, halv...  9.69 us
    pallas_call x2, Pallas kernels, weight_grads(): pl.pallas_call(functools.partial(grads_kernel, slots, tile, by_rows), out...  9.59 us
    ppermute x13, waiting for transfers between devices, exchanged(): lax.ppermute(pieces[i], 'ep', [(j, j ^ i * step) for j in peers])  5.77 us
    ppermute x2, starting transfers between devices, beside(): lax.ppermute(value, 'section', [(i, j if 0 <= j < size else i) for i, j i...  4.55 us
    pallas_call x1, Pallas kernels, loaded(): pl.pallas_call(functools.partial(load_kernel, amount), out_shape=tuple((h...  3.24 us
    ppermute x2, starting transfers between devices, swapped(): lax.ppermute(halves[1], 'ep', [(j, j ^ 1) for j in peers])  2.78 us
    pallas_call x1, Pallas kernels, body(): pl.pallas_call(functools.partial(early_kernel, capacity, groups), out_sha...  2.07 us
  transfers between devices with their start and end apart: 17, of which 5 were waited for; matrix products, arithmetic and copies ran while one was open for 0% of the time, Pallas kernels for 25%

profile of v4, /device:TPU:9, one launch (start us, length us, event | category | flops | bytes accessed | tf_op | source)
XLA Modules:
  0.0 56.1 jit_solution(14094459856830232142)
XLA Ops:
  0.6 0.1 pad_add_fusion.place_ref
  0.7 2.1 %early_rows.1 = (bf16[16,3584]{1,0:T(8,128)(2,1)S(1)}, bf16[16,3584]{1,0:T(8,128)(2,1)S(1)}, bf16[16,3584]{1,0:T(8,128)(2,1)S(1)}, bf16[16,3584]{1,0:T(8,128)(2,...) custom-call(s32[4]{0:T(128)S(1)} %pad_add_fusion.place_ref, ...), custom_call_target="tpu_custom_call" | custom-call | flops 7340032 | bytes 458752 | tf_op jit(solution)/shard_map/early_rows/pallas_call | solution.py:437
  2.8 0.1 collective-permute-start
  2.9 4.5 %collective-permute-start.1 = (bf16[16,3584]{1,0:T(8,128)(2,1)S(1)}, bf16[16,3584]{1,0:T(8,128)(2,1)S(1)}, u32[]{:S(2)}, u32[]{:S(2)}) collective-permute-start(bf16[16,3584]{1,0:T(8,128)(2,1)S(1)} %get-tuple-element.49), channel_id=1, source_target_pairs={{0,0},{8,16},{16,8},{24,24},{1,1},{9,17},{17,9},{25,25},{2,2},{10,... | collective-permute-start | bytes 344072 | tf_op jit(solution)/shard_map/ppermute | solution.py:406
  7.4 1.3 %collective-permute-start.9 = (bf16[16,3584]{1,0:T(8,128)(2,1)S(1)}, bf16[16,3584]{1,0:T(8,128)(2,1)S(1)}, u32[]{:S(2)}, u32[]{:S(2)}) collective-permute-start(bf16[16,3584]{1,0:T(8,128)(2,1)S(1)} %get-tuple-element.71), channel_id=1, source_target_pairs={{0,2},{1,3},{2,0},{3,1},{4,6},{5,7},{6,4},{7,5},{8,10},{9,11},{10,... | collective-permute-start | bytes 344072 | tf_op jit(solution)/shard_map/ppermute | solution.py:343
  8.6 1.2 %collective-permute-start.10 = (bf16[16,3584]{1,0:T(8,128)(2,1)S(1)}, bf16[16,3584]{1,0:T(8,128)(2,1)S(1)}, u32[]{:S(2)}, u32[]{:S(2)}) collective-permute-start(bf16[16,3584]{1,0:T(8,128)(2,1)S(1)} %get-tuple-element.72), channel_id=1, source_target_pairs={{0,4},{1,5},{2,6},{3,7},{4,0},{5,1},{6,2},{7,3},{8,12},{9,13},{10,... | collective-permute-start | bytes 344072 | tf_op jit(solution)/shard_map/ppermute | solution.py:343
  9.9 0.2 collective-permute-start.11
  10.1 0.0 collective-permute-done.even_ref
  10.1 0.0 collective-permute-done.1.odd_ref
  10.1 1.1 %pack_rows.1 = (bf16[16,3584]{1,0:T(8,128)(2,1)S(1)}, bf16[16,3584]{1,0:T(8,128)(2,1)S(1)}, bf16[8,7168]{1,0:T(8,128)(2,1)S(1)}, bf16[8,7168]{1,0:T(8,128)(2,1)S...) custom-call(s32[4]{0:T(128)S(1)} %pad_add_fusion.place_ref, ...), custom_call_target="tpu_custom_call" | custom-call | flops 29360128 | bytes 1146880 | tf_op jit(solution)/shard_map/pack_rows/pallas_call | solution.py:468
  11.2 3.2 %collective-permute-start.2 = (bf16[8,7168]{1,0:T(8,128)(2,1)S(1)}, bf16[8,7168]{1,0:T(8,128)(2,1)S(1)}, u32[]{:S(2)}, u32[]{:S(2)}) collective-permute-start(bf16[8,7168]{1,0:T(8,128)(2,1)S(1)} %get-tuple-element.62), channel_id=1, source_target_pairs={{0,3},{1,2},{2,1},{3,0},{4,7},{5,6},{6,5},{7,4},{8,11},{9,10},{10,... | collective-permute-start | bytes 344072 | tf_op jit(solution)/shard_map/ppermute | solution.py:343
  14.4 0.0 collective-permute-start.3
  14.4 0.0 collective-permute-done.9.refs_1_
  14.4 0.3 collective-permute-start.4
  14.7 0.0 collective-permute-done.10.refs_2_
  14.7 0.3 collective-permute-done.11.refs_3_
  15.0 0.1 split_rows.1
  15.1 2.5 %collective-permute-start.12 = (bf16[32,3584]{1,0:T(8,128)(2,1)S(1)}, bf16[32,3584]{1,0:T(8,128)(2,1)S(1)}, u32[]{:S(2)}, u32[]{:S(2)}) collective-permute-start(bf16[32,3584]{1,0:T(8,128)(2,1)S(1)} %get-tuple-element.75), channel_id=1, source_target_pairs={{0,1},{1,0},{2,3},{3,2},{4,5},{5,4},{6,7},{7,6},{8,9},{9,8},{10,11... | collective-permute-start | bytes 688136 | tf_op jit(solution)/shard_map/ppermute | solution.py:351
  17.6 0.8 %collective-permute-start.5 = (bf16[8,7168]{1,0:T(8,128)(2,1)S(1)}, bf16[8,7168]{1,0:T(8,128)(2,1)S(1)}, u32[]{:S(2)}, u32[]{:S(2)}) collective-permute-start(bf16[8,7168]{1,0:T(8,128)(2,1)S(1)} %get-tuple-element.66), channel_id=1, source_target_pairs={{0,4},{1,5},{2,6},{3,7},{4,0},{5,1},{6,2},{7,3},{8,12},{9,13},{10,... | collective-permute-start | bytes 344072 | tf_op jit(solution)/shard_map/ppermute | solution.py:343
  18.4 0.0 collective-permute-done.2.refs_0_.refs_3_
  18.4 1.5 %collective-permute-start.6 = (bf16[8,7168]{1,0:T(8,128)(2,1)S(1)}, bf16[8,7168]{1,0:T(8,128)(2,1)S(1)}, u32[]{:S(2)}, u32[]{:S(2)}) collective-permute-start(bf16[8,7168]{1,0:T(8,128)(2,1)S(1)} %get-tuple-element.67), channel_id=1, source_target_pairs={{0,5},{1,4},{2,7},{3,6},{4,1},{5,0},{6,3},{7,2},{8,13},{9,12},{10,... | collective-permute-start | bytes 344072 | tf_op jit(solution)/shard_map/ppermute | solution.py:343
  19.9 0.0 collective-permute-done.3.refs_1_
  19.9 0.5 collective-permute-start.7
  20.5 0.4 collective-permute-done.4.refs_2_
  20.8 1.7 %collective-permute-start.8 = (bf16[8,7168]{1,0:T(8,128)(2,1)S(1)}, bf16[8,7168]{1,0:T(8,128)(2,1)S(1)}, u32[]{:S(2)}, u32[]{:S(2)}) collective-permute-start(bf16[8,7168]{1,0:T(8,128)(2,1)S(1)} %get-tuple-element.69), channel_id=1, source_target_pairs={{0,7},{1,6},{2,5},{3,4},{4,3},{5,2},{6,1},{7,0},{8,15},{9,14},{10,... | collective-permute-start | bytes 344072 | tf_op jit(solution)/shard_map/ppermute | solution.py:343
  22.6 3.2 %load_weights.1.gate_ref = bf16[3584,1024]{1,0:T(8,128)(2,1)S(1)} custom-call(bf16[8,7168]{1,0:T(8,128)(2,1)S(1)} %collective-permute-done.2.refs_0_.refs_3_, bf16[3584,1024]{1,0:T(8,128)(2,1)} %bitcast.43), custom_call_target="tpu_custom_call" | custom-call | bytes 7340032 | tf_op jit(solution)/shard_map/load_weights/pallas_call | solution.py:324
  25.8 0.0 collective-permute-done.5.refs_4_
  25.8 4.0 %collective-permute-done.6.refs_5_ = bf16[8,7168]{1,0:T(8,128)(2,1)S(1)} collective-permute-done((bf16[8,7168]{1,0:T(8,128)(2,1)S(1)}, bf16[8,7168]{1,0:T(8,128)(2,1)S(1)}, u32[]{:S(2)}, u32[]{:S(2)}) %collective-permute-start.6) | collective-permute-done | bytes 114720 | tf_op jit(solution)/shard_map/ppermute | solution.py:343
  29.8 0.0 collective-permute-done.7.refs_6_
  29.8 0.0 collective-permute-done.8.refs_7_
  29.8 0.0 collective-permute-done.12.refs_9_
  29.9 0.0 slice-done
  29.9 0.0 slice-done.1
  29.9 0.0 slice-start.3
  29.9 0.0 slice-start.7
  29.9 9.7 %expert_rows.1 = (bf16[64,3584]{1,0:T(8,128)(2,1)S(1)}, bf16[3584,64]{1,0:T(8,128)(2,1)S(1)}, bf16[1024,64]{1,0:T(8,128)(2,1)S(1)}, bf16[64,1024]{1,0:T(8,128)(2...) custom-call(bf16[3584,1024]{1,0:T(8,128)(2,1)S(1)} %load_weights.1.gate_ref, ...), custom_call_target="tpu_custom_call" | custom-call | flops 3758096384 | bytes 22020096 | tf_op jit(solution)/shard_map/expert_rows/pallas_call | solution.py:491
  39.6 0.3 collective-permute-start.13
  39.9 1.6 %collective-permute-done.13.arrived_ref = bf16[32,7168]{1,0:T(8,128)(2,1)S(1)} collective-permute-done((bf16[32,7168]{1,0:T(8,128)(2,1)S(1)}, bf16[32,7168]{1,0:T(8,128)(2,1)S(1)}, u32[]{:S(2)}, u32[]{:S(2)}) %collective-permute-start.13) | collective-permute-done | bytes 458784 | tf_op jit(solution)/shard_map/ppermute | solution.py:351
  41.5 0.1 merge_rows.1
  41.6 0.7 %collective-permute-start.14 = (bf16[16,7168]{1,0:T(8,128)(2,1)S(1)}, bf16[16,7168]{1,0:T(8,128)(2,1)S(1)}, u32[]{:S(2)}, u32[]{:S(2)}) collective-permute-start(bf16[16,7168]{1,0:T(8,128)(2,1)S(1)} %get-tuple-element.79), channel_id=1, source_target_pairs={{0,6},{1,7},{2,4},{3,5},{4,2},{5,3},{6,0},{7,1},{8,14},{9,15},{10,... | collective-permute-start | bytes 688136 | tf_op jit(solution)/shard_map/ppermute | solution.py:343
  42.3 1.3 %collective-permute-start.15 = (bf16[16,7168]{1,0:T(8,128)(2,1)S(1)}, bf16[16,7168]{1,0:T(8,128)(2,1)S(1)}, u32[]{:S(2)}, u32[]{:S(2)}) collective-permute-start(bf16[16,7168]{1,0:T(8,128)(2,1)S(1)} %get-tuple-element.80), channel_id=1, source_target_pairs={{0,2},{1,3},{2,0},{3,1},{4,6},{5,7},{6,4},{7,5},{8,10},{9,11},{10,... | collective-permute-start | bytes 688136 | tf_op jit(solution)/shard_map/ppermute | solution.py:343
  43.6 0.7 %collective-permute-start.16 = (bf16[16,7168]{1,0:T(8,128)(2,1)S(1)}, bf16[16,7168]{1,0:T(8,128)(2,1)S(1)}, u32[]{:S(2)}, u32[]{:S(2)}) collective-permute-start(bf16[16,7168]{1,0:T(8,128)(2,1)S(1)} %get-tuple-element.81), channel_id=1, source_target_pairs={{0,4},{1,5},{2,6},{3,7},{4,0},{5,1},{6,2},{7,3},{8,12},{9,13},{10,... | collective-permute-start | bytes 688136 | tf_op jit(solution)/shard_map/ppermute | solution.py:343
  44.4 3.5 %weight_grads.2 = bf16[3584,1024]{1,0:T(8,128)(2,1)} custom-call(bf16[32,7168]{1,0:T(8,128)(2,1)S(1)} %get-tuple-element.76.keep_ref.after_hbm, bf16[3584,1024]{1,0:T(8,128)(2,1)S(1)} %bitcast.36, bf16[3584,64]{1,0:T(8,128)(2,1)S(1)} %get-tuple-element.84.refs_1_.refs_2_, bf16[64,1024]{1,0:T(8,128)(2,1)S(1)} %get-tuple-element.85.refs_2_), custom_call_target="tpu_custom_call" | custom-call | flops 469762048 | bytes 14680064 | tf_op jit(solution)/shard_map/weight_grads/pallas_call | solution.py:390
  47.9 6.1 %weight_grads.3 = (bf16[3584,1024]{1,0:T(8,128)(2,1)}, bf16[1024,3584]{1,0:T(8,128)(2,1)}) custom-call(bf16[16,7168]{1,0:T(8,128)(2,1)S(1)} %get-tuple-element.78.refs_0_.after_hbm, bf16[3584,1024]{1,0:T(8,128)(2,1)S(1)} %bitcast.39, bf16[1024,3584]{1,0:T(8,128)(2,1)S(1)} %bitcast.42, bf16[3584,64]{1,0:T(8,128)(2,1)S(1)} %get-tuple-element.84.refs_1_.refs_2_, ...), custom_call_target="tpu_custom_call" | custom-call | flops 939524096 | bytes 29360128 | tf_op jit(solution)/shard_map/weight_grads/pallas_call | solution.py:390
  54.0 0.0 collective-permute-done.14.refs_1_
  54.0 0.0 collective-permute-done.15.refs_2_
  54.1 1.0 %collective-permute-done.16.refs_3_ = bf16[16,7168]{1,0:T(8,128)(2,1)S(1)} collective-permute-done((bf16[16,7168]{1,0:T(8,128)(2,1)S(1)}, bf16[16,7168]{1,0:T(8,128)(2,1)S(1)}, u32[]{:S(2)}, u32[]{:S(2)}) %collective-permute-start.16) | collective-permute-done | bytes 229408 | tf_op jit(solution)/shard_map/ppermute | solution.py:343
  55.0 1.1 %combine_rows.1 = (bf16[16,3584]{1,0:T(8,128)(2,1)}, bf16[16,3584]{1,0:T(8,128)(2,1)}) custom-call(bf16[16,3584]{1,0:T(8,128)(2,1)S(1)} %get-tuple-element.56.front_ref, bf16[16,3584]{1,0:T(8,128)(2,1)S(1)} %get-tuple-element.57.upstream_ref, bf16[16,3584]{1,0:T(8,128)(2,1)S(1)} %get-tuple-element.58.saved_ref, ...), custom_call_target="tpu_custom_call" | custom-call | flops 22020096 | bytes 917504 | tf_op jit(solution)/shard_map/combine_rows/pallas_call | solution.py:520
  (18 shorter events, 0.0 us)
Async XLA Ops:
  2.8 7.3 %collective-permute-start = (bf16[16,3584]{1,0:T(8,128)(2,1)S(1)}, bf16[16,3584]{1,0:T(8,128)(2,1)S(1)}, u32[]{:S(2)}, u32[]{:S(2)}) collective-permute-start(bf16[16,3584]{1,0:T(8,128)(2,1)S(1)} %get-tuple-element.48), channel_id=1, source_target_pairs={{0,8},{8,0},{16,24},{24,16},{1,9},{9,1},{17,25},{25,17},{2,10},{10... | collective-permute-start | bytes 344072 | tf_op jit(solution)/shard_map/ppermute | solution.py:406
  2.9 7.2 %collective-permute-start.1 = (bf16[16,3584]{1,0:T(8,128)(2,1)S(1)}, bf16[16,3584]{1,0:T(8,128)(2,1)S(1)}, u32[]{:S(2)}, u32[]{:S(2)}) collective-permute-start(bf16[16,3584]{1,0:T(8,128)(2,1)S(1)} %get-tuple-element.49), channel_id=1, source_target_pairs={{0,0},{8,16},{16,8},{24,24},{1,1},{9,17},{17,9},{25,25},{2,2},{10,... | collective-permute-start | bytes 344072 | tf_op jit(solution)/shard_map/ppermute | solution.py:406
  7.4 7.1 %collective-permute-start.9 = (bf16[16,3584]{1,0:T(8,128)(2,1)S(1)}, bf16[16,3584]{1,0:T(8,128)(2,1)S(1)}, u32[]{:S(2)}, u32[]{:S(2)}) collective-permute-start(bf16[16,3584]{1,0:T(8,128)(2,1)S(1)} %get-tuple-element.71), channel_id=1, source_target_pairs={{0,2},{1,3},{2,0},{3,1},{4,6},{5,7},{6,4},{7,5},{8,10},{9,11},{10,... | collective-permute-start | bytes 344072 | tf_op jit(solution)/shard_map/ppermute | solution.py:343
  8.6 6.0 %collective-permute-start.10 = (bf16[16,3584]{1,0:T(8,128)(2,1)S(1)}, bf16[16,3584]{1,0:T(8,128)(2,1)S(1)}, u32[]{:S(2)}, u32[]{:S(2)}) collective-permute-start(bf16[16,3584]{1,0:T(8,128)(2,1)S(1)} %get-tuple-element.72), channel_id=1, source_target_pairs={{0,4},{1,5},{2,6},{3,7},{4,0},{5,1},{6,2},{7,3},{8,12},{9,13},{10,... | collective-permute-start | bytes 344072 | tf_op jit(solution)/shard_map/ppermute | solution.py:343
  9.9 5.1 %collective-permute-start.11 = (bf16[16,3584]{1,0:T(8,128)(2,1)S(1)}, bf16[16,3584]{1,0:T(8,128)(2,1)S(1)}, u32[]{:S(2)}, u32[]{:S(2)}) collective-permute-start(bf16[16,3584]{1,0:T(8,128)(2,1)S(1)} %get-tuple-element.73), channel_id=1, source_target_pairs={{0,6},{1,7},{2,4},{3,5},{4,2},{5,3},{6,0},{7,1},{8,14},{9,15},{10,... | collective-permute-start | bytes 344072 | tf_op jit(solution)/shard_map/ppermute | solution.py:343
  11.2 7.2 %collective-permute-start.2 = (bf16[8,7168]{1,0:T(8,128)(2,1)S(1)}, bf16[8,7168]{1,0:T(8,128)(2,1)S(1)}, u32[]{:S(2)}, u32[]{:S(2)}) collective-permute-start(bf16[8,7168]{1,0:T(8,128)(2,1)S(1)} %get-tuple-element.62), channel_id=1, source_target_pairs={{0,3},{1,2},{2,1},{3,0},{4,7},{5,6},{6,5},{7,4},{8,11},{9,10},{10,... | collective-permute-start | bytes 344072 | tf_op jit(solution)/shard_map/ppermute | solution.py:343
  14.4 5.5 %collective-permute-start.3 = (bf16[8,7168]{1,0:T(8,128)(2,1)S(1)}, bf16[8,7168]{1,0:T(8,128)(2,1)S(1)}, u32[]{:S(2)}, u32[]{:S(2)}) collective-permute-start(bf16[8,7168]{1,0:T(8,128)(2,1)S(1)} %get-tuple-element.64), channel_id=1, source_target_pairs={{0,1},{1,0},{2,3},{3,2},{4,5},{5,4},{6,7},{7,6},{8,9},{9,8},{10,11... | collective-permute-start | bytes 344072 | tf_op jit(solution)/shard_map/ppermute | solution.py:343
  14.4 6.4 %collective-permute-start.4 = (bf16[8,7168]{1,0:T(8,128)(2,1)S(1)}, bf16[8,7168]{1,0:T(8,128)(2,1)S(1)}, u32[]{:S(2)}, u32[]{:S(2)}) collective-permute-start(bf16[8,7168]{1,0:T(8,128)(2,1)S(1)} %get-tuple-element.65), channel_id=1, source_target_pairs={{0,2},{1,3},{2,0},{3,1},{4,6},{5,7},{6,4},{7,5},{8,10},{9,11},{10,... | collective-permute-start | bytes 344072 | tf_op jit(solution)/shard_map/ppermute | solution.py:343
  15.0 14.8 %slice-start = ((s8[7340032]{0:T(1024)(128)(4,1)}), s8[4194304]{0:T(1024)(128)(4,1)S(1)}, s32[]{:S(2)}) async-start(s8[7340032]{0:T(1024)(128)(4,1)} %bitcast.30), calls=%async_computation | async-start | bytes 8388608
  15.1 14.8 %collective-permute-start.12 = (bf16[32,3584]{1,0:T(8,128)(2,1)S(1)}, bf16[32,3584]{1,0:T(8,128)(2,1)S(1)}, u32[]{:S(2)}, u32[]{:S(2)}) collective-permute-start(bf16[32,3584]{1,0:T(8,128)(2,1)S(1)} %get-tuple-element.75), channel_id=1, source_target_pairs={{0,1},{1,0},{2,3},{3,2},{4,5},{5,4},{6,7},{7,6},{8,9},{9,8},{10,11... | collective-permute-start | bytes 688136 | tf_op jit(solution)/shard_map/ppermute | solution.py:351
  17.6 8.3 %collective-permute-start.5 = (bf16[8,7168]{1,0:T(8,128)(2,1)S(1)}, bf16[8,7168]{1,0:T(8,128)(2,1)S(1)}, u32[]{:S(2)}, u32[]{:S(2)}) collective-permute-start(bf16[8,7168]{1,0:T(8,128)(2,1)S(1)} %get-tuple-element.66), channel_id=1, source_target_pairs={{0,4},{1,5},{2,6},{3,7},{4,0},{5,1},{6,2},{7,3},{8,12},{9,13},{10,... | collective-permute-start | bytes 344072 | tf_op jit(solution)/shard_map/ppermute | solution.py:343
  18.4 11.4 %collective-permute-start.6 = (bf16[8,7168]{1,0:T(8,128)(2,1)S(1)}, bf16[8,7168]{1,0:T(8,128)(2,1)S(1)}, u32[]{:S(2)}, u32[]{:S(2)}) collective-permute-start(bf16[8,7168]{1,0:T(8,128)(2,1)S(1)} %get-tuple-element.67), channel_id=1, source_target_pairs={{0,5},{1,4},{2,7},{3,6},{4,1},{5,0},{6,3},{7,2},{8,13},{9,12},{10,... | collective-permute-start | bytes 344072 | tf_op jit(solution)/shard_map/ppermute | solution.py:343
  19.9 9.9 %collective-permute-start.7 = (bf16[8,7168]{1,0:T(8,128)(2,1)S(1)}, bf16[8,7168]{1,0:T(8,128)(2,1)S(1)}, u32[]{:S(2)}, u32[]{:S(2)}) collective-permute-start(bf16[8,7168]{1,0:T(8,128)(2,1)S(1)} %get-tuple-element.68), channel_id=1, source_target_pairs={{0,6},{1,7},{2,4},{3,5},{4,2},{5,3},{6,0},{7,1},{8,14},{9,15},{10,... | collective-permute-start | bytes 344072 | tf_op jit(solution)/shard_map/ppermute | solution.py:343
  20.8 9.0 %collective-permute-start.8 = (bf16[8,7168]{1,0:T(8,128)(2,1)S(1)}, bf16[8,7168]{1,0:T(8,128)(2,1)S(1)}, u32[]{:S(2)}, u32[]{:S(2)}) collective-permute-start(bf16[8,7168]{1,0:T(8,128)(2,1)S(1)} %get-tuple-element.69), channel_id=1, source_target_pairs={{0,7},{1,6},{2,5},{3,4},{4,3},{5,2},{6,1},{7,0},{8,15},{9,14},{10,... | collective-permute-start | bytes 344072 | tf_op jit(solution)/shard_map/ppermute | solution.py:343
  22.6 7.3 %slice-start.1 = ((s8[7340032]{0:T(1024)(128)(4,1)}), s8[3145728]{0:T(1024)(128)(4,1)S(1)}, s32[]{:S(2)}) async-start(s8[7340032]{0:T(1024)(128)(4,1)} %bitcast.30), calls=%async_computation.1 | async-start | bytes 6291456
  22.6 7.3 %copy-start = (bf16[1,1024,3584]{2,1,0:T(8,128)(2,1)S(1)}, bf16[1,1024,3584]{2,1,0:T(8,128)(2,1)}, u32[]{:S(2)}) copy-start(bf16[1,1024,3584]{2,1,0:T(8,128)(2,1)} %param.28) | copy-start | bytes 22020100
  22.6 21.8 %slice-start.2 = ((s8[7340032]{0:T(1024)(128)(4,1)}), s8[4194304]{0:T(1024)(128)(4,1)S(1)}, s32[]{:S(2)}) async-start(s8[7340032]{0:T(1024)(128)(4,1)} %bitcast.34), calls=%async_computation.2 | async-start | bytes 8388608
  22.6 25.3 %slice-start.6 = ((s8[7340032]{0:T(1024)(128)(4,1)}), s8[4194304]{0:T(1024)(128)(4,1)S(1)}, s32[]{:S(2)}) async-start(s8[7340032]{0:T(1024)(128)(4,1)} %bitcast.40), calls=%async_computation.6 | async-start | bytes 8388608
  29.9 14.5 %slice-start.3 = ((s8[7340032]{0:T(1024)(128)(4,1)}), s8[3145728]{0:T(1024)(128)(4,1)S(1)}, s32[]{:S(2)}) async-start(s8[7340032]{0:T(1024)(128)(4,1)} %bitcast.34), calls=%async_computation.3 | async-start | bytes 6291456
  29.9 18.0 %slice-start.7 = ((s8[7340032]{0:T(1024)(128)(4,1)}), s8[3145728]{0:T(1024)(128)(4,1)S(1)}, s32[]{:S(2)}) async-start(s8[7340032]{0:T(1024)(128)(4,1)} %bitcast.40), calls=%async_computation.7 | async-start | bytes 6291456
  39.6 1.9 %collective-permute-start.13 = (bf16[32,7168]{1,0:T(8,128)(2,1)S(1)}, bf16[32,7168]{1,0:T(8,128)(2,1)S(1)}, u32[]{:S(2)}, u32[]{:S(2)}) collective-permute-start(bf16[32,7168]{1,0:T(8,128)(2,1)S(1)} %get-tuple-element.77), channel_id=1, source_target_pairs={{0,1},{1,0},{2,3},{3,2},{4,5},{5,4},{6,7},{7,6},{8,9},{9,8},{10,11... | collective-permute-start | bytes 1376264 | tf_op jit(solution)/shard_map/ppermute | solution.py:351
  41.5 6.4 %slice-start.4 = ((s8[7340032]{0:T(1024)(128)(4,1)}), s8[4194304]{0:T(1024)(128)(4,1)S(1)}, s32[]{:S(2)}) async-start(s8[7340032]{0:T(1024)(128)(4,1)} %bitcast.37), calls=%async_computation.4 | async-start | bytes 8388608
  41.6 12.4 %collective-permute-start.14 = (bf16[16,7168]{1,0:T(8,128)(2,1)S(1)}, bf16[16,7168]{1,0:T(8,128)(2,1)S(1)}, u32[]{:S(2)}, u32[]{:S(2)}) collective-permute-start(bf16[16,7168]{1,0:T(8,128)(2,1)S(1)} %get-tuple-element.79), channel_id=1, source_target_pairs={{0,6},{1,7},{2,4},{3,5},{4,2},{5,3},{6,0},{7,1},{8,14},{9,15},{10,... | collective-permute-start | bytes 688136 | tf_op jit(solution)/shard_map/ppermute | solution.py:343
  42.3 11.7 %collective-permute-start.15 = (bf16[16,7168]{1,0:T(8,128)(2,1)S(1)}, bf16[16,7168]{1,0:T(8,128)(2,1)S(1)}, u32[]{:S(2)}, u32[]{:S(2)}) collective-permute-start(bf16[16,7168]{1,0:T(8,128)(2,1)S(1)} %get-tuple-element.80), channel_id=1, source_target_pairs={{0,2},{1,3},{2,0},{3,1},{4,6},{5,7},{6,4},{7,5},{8,10},{9,11},{10,... | collective-permute-start | bytes 688136 | tf_op jit(solution)/shard_map/ppermute | solution.py:343
  43.6 11.4 %collective-permute-start.16 = (bf16[16,7168]{1,0:T(8,128)(2,1)S(1)}, bf16[16,7168]{1,0:T(8,128)(2,1)S(1)}, u32[]{:S(2)}, u32[]{:S(2)}) collective-permute-start(bf16[16,7168]{1,0:T(8,128)(2,1)S(1)} %get-tuple-element.81), channel_id=1, source_target_pairs={{0,4},{1,5},{2,6},{3,7},{4,0},{5,1},{6,2},{7,3},{8,12},{9,13},{10,... | collective-permute-start | bytes 688136 | tf_op jit(solution)/shard_map/ppermute | solution.py:343
  44.4 3.6 %slice-start.5 = ((s8[7340032]{0:T(1024)(128)(4,1)}), s8[3145728]{0:T(1024)(128)(4,1)S(1)}, s32[]{:S(2)}) async-start(s8[7340032]{0:T(1024)(128)(4,1)} %bitcast.37), calls=%async_computation.5 | async-start | bytes 6291456
